TPU v7x, 512 devices: a whole 4x8x8 slice. The times are simulated.
512 devices in a mesh: blk: 128 (over x, z_lo, y), heads: 4 (over z_hi, core).
Axes of the slice: x: 4, y: 8, z: 8 (z_hi: 2, z_lo: 4; z = z_hi * 4 + z_lo), core: 2. Of those that a mesh axis runs over, the one named last changes fastest.
Arguments:
- queries: bfloat16 [32768, 4096], P('blk', 'heads'), may hold values from -5 to 5
- keys: bfloat16 [32768, 1024], P('blk', 'heads'), may hold values from -5 to 5
- values: bfloat16 [32768, 1024], P('blk', 'heads'), may hold values from -6 to 6
- doc_ids: int32 [32768], P('blk'), may hold values from 0 to 127, never falling along the last dimension, each value on 1 to 1024 neighbouring positions
Outputs:
- attended: bfloat16 [32768, 4096], P('blk', 'heads')
Inputs may be any that keep to these rules, and one draw needn't show every extreme that they name: `doc_ids`: Non-decreasing along the sequence; every document has 1024 tokens at most, and some document exactly 1024.
All inputs are finite; a program needn't handle non-finite values.
Results may differ from a plain program's by a relative error of at most 0.0034.
Values may be sent and summed in bfloat16 or wider, within the bound.
No kernel may reach another device: no remote copies, remote signals or barrier semaphores. Data moves between devices by JAX's collectives and lax.ppermute only.
A program may use at most 64 MiB of HBM per device.

v0:
```python
import math

import jax
import jax.numpy as jnp
from jax import lax
from jax.sharding import PartitionSpec as P

HEAD_WIDTH = 128
DOC_BLKS = 4


def shifted(value, axis, steps):
    count = lax.axis_size(axis)
    initial, last = (max(0, -steps), min(count, count - steps))
    return lax.ppermute(value, axis, [(source, source + steps) for source in range(initial, last)])


def shards(queries, keys, values, doc_ids):
    row_count = queries.shape[0]
    kv_heads = keys.shape[1] // HEAD_WIDTH
    queries_per_group = queries.shape[1] // keys.shape[1]
    score_scale = 1.0 / math.sqrt(HEAD_WIDTH)
    device_index = lax.axis_index("blk")
    query_heads = queries.reshape(row_count, kv_heads, queries_per_group, HEAD_WIDTH)
    row_numbers = jnp.arange(row_count, dtype=jnp.int32)
    causal = row_numbers[None, :] <= row_numbers[:, None]
    own_block = (keys, values, doc_ids)
    blocks = [(own_block, 0)]
    for offset in range(1, DOC_BLKS + 1):
        blocks.append((shifted((own_block[0], own_block[1], own_block[2]), "blk", offset), offset))
    empty_sum = jnp.zeros((kv_heads, queries_per_group, row_count), jnp.float32)
    empty_num = jnp.zeros((row_count, kv_heads, queries_per_group, HEAD_WIDTH), jnp.float32)
    kept_scores = []
    rowmax = jnp.full((kv_heads, queries_per_group, row_count), -jnp.inf, jnp.float32)
    for received, offset in blocks:
        block_of_keys, block_of_values, key_docs = received
        key_heads = block_of_keys.reshape(row_count, kv_heads, HEAD_WIDTH)
        scores = (
            jnp.einsum("qkgd,skd->kgqs", query_heads, key_heads, preferred_element_type=jnp.float32)
            * score_scale
        )
        allowed = (doc_ids[:, None] == key_docs[None, :]) & (device_index >= offset)
        if offset == 0:
            allowed = allowed & causal
        scores = jnp.where(allowed, scores, -jnp.inf)
        kept_scores.append(scores)
        rowmax = jnp.maximum(rowmax, jnp.max(scores, axis=-1))
    denominator = empty_sum
    numerator = empty_num
    for (received, offset), scores in zip(blocks, kept_scores):
        weights = jnp.exp(scores - rowmax[..., None])
        value_heads = received[1].reshape(row_count, kv_heads, HEAD_WIDTH)
        block_numerator = jnp.einsum(
            "kgqs,skd->qkgd",
            weights.astype(jnp.bfloat16),
            value_heads,
            preferred_element_type=jnp.float32,
        )
        partial_den = jnp.sum(weights, axis=-1)
        denominator = denominator + partial_den
        numerator = numerator + block_numerator
    result = numerator / jnp.transpose(denominator, (2, 0, 1))[..., None]
    return result.reshape(row_count, kv_heads * queries_per_group * HEAD_WIDTH).astype(jnp.bfloat16)


def solution(mesh):
    return jax.shard_map(
        shards,
        mesh=mesh,
        in_specs=(P("blk", "heads"), P("blk", "heads"), P("blk", "heads"), P("blk")),
        out_specs=P("blk", "heads"),
        check_vma=False,
    )
```

profile of v0, /device:TPU:260, one launch (start us, length us, event | category | flops | bytes accessed | tf_op | source)
XLA Modules:
  0.0 92.8 jit_solution(11161822074150173641)
XLA Ops:
  0.0 3.5 %collective-permute-start = (s32[256]{0:T(256)}, s32[256]{0:T(256)S(1)}, u32[]{:S(2)}, u32[]{:S(2)}) collective-permute-start(s32[256]{0:T(256)} %param.7), channel_id=1, source_target_pairs={{0,4},{4,8},{8,12},{12,16},{16,20},{20,24},{24,28},{28,32},{32,36}... | collective-permute-start | bytes 3080 | tf_op jit(solution)/shard_map/ppermute | solution.py:15
  3.5 4.5 %collective-permute-start.2 = (s32[256]{0:T(256)}, s32[256]{0:T(256)S(1)}, u32[]{:S(2)}, u32[]{:S(2)}) collective-permute-start(s32[256]{0:T(256)} %param.7), channel_id=1, source_target_pairs={{0,8},{4,12},{8,16},{12,20},{16,24},{20,28},{24,32},{28,36},{32,40... | collective-permute-start | bytes 3080 | tf_op jit(solution)/shard_map/ppermute | solution.py:15
  8.0 4.9 %collective-permute-start.4 = (s32[256]{0:T(256)}, s32[256]{0:T(256)S(1)}, u32[]{:S(2)}, u32[]{:S(2)}) collective-permute-start(s32[256]{0:T(256)} %param.7), channel_id=1, source_target_pairs={{0,12},{4,16},{8,20},{12,24},{16,28},{20,32},{24,36},{28,40},{32,4... | collective-permute-start | bytes 3080 | tf_op jit(solution)/shard_map/ppermute | solution.py:15
  12.9 4.7 %collective-permute-start.6 = (s32[256]{0:T(256)}, s32[256]{0:T(256)S(1)}, u32[]{:S(2)}, u32[]{:S(2)}) collective-permute-start(s32[256]{0:T(256)} %param.7), channel_id=1, source_target_pairs={{0,16},{4,20},{8,24},{12,28},{16,32},{20,36},{24,40},{28,44},{32,4... | collective-permute-start | bytes 3080 | tf_op jit(solution)/shard_map/ppermute | solution.py:15
  17.7 1.7 %copy.24 = bf16[256,256]{0,1:T(8,128)(2,1)} copy(bf16[256,256]{1,0:T(8,128)(2,1)} %param.5) | data formatting | bytes 262144 | tf_op args[1]
  19.3 5.9 %collective-permute-start.7 = (bf16[256,256]{0,1:T(8,128)(2,1)}, bf16[256,256]{0,1:T(8,128)(2,1)S(1)}, u32[]{:S(2)}, u32[]{:S(2)}) collective-permute-start(bf16[256,256]{0,1:T(8,128)(2,1)} %copy.24), channel_id=1, source_target_pairs={{0,16},{4,20},{8,24},{12,28},{16,32},{20,36},{24,40},{28,44},{32,4... | collective-permute-start | bytes 393224 | tf_op jit(solution)/shard_map/ppermute | solution.py:15
  26.2 1.4 %reshape.57 = bf16[256,2,4,128]{3,2,1,0:T(4,128)(2,1)S(1)} reshape(bf16[256,1024]{1,0:T(8,128)(2,1)} %param.4) | data formatting | bytes 1048576 | tf_op jit(solution)/shard_map/reshape | solution.py:24
  28.7 3.7 %collective-permute-start.5 = (bf16[256,256]{0,1:T(8,128)(2,1)}, bf16[256,256]{0,1:T(8,128)(2,1)S(1)}, u32[]{:S(2)}, u32[]{:S(2)}) collective-permute-start(bf16[256,256]{0,1:T(8,128)(2,1)} %copy.24), channel_id=1, source_target_pairs={{0,12},{4,16},{8,20},{12,24},{16,28},{20,32},{24,36},{28,40},{32,4... | collective-permute-start | bytes 393224 | tf_op jit(solution)/shard_map/ppermute | solution.py:15
  32.4 4.5 %collective-permute-start.3 = (bf16[256,256]{0,1:T(8,128)(2,1)}, bf16[256,256]{0,1:T(8,128)(2,1)S(1)}, u32[]{:S(2)}, u32[]{:S(2)}) collective-permute-start(bf16[256,256]{0,1:T(8,128)(2,1)} %copy.24), channel_id=1, source_target_pairs={{0,8},{4,12},{8,16},{12,20},{16,24},{20,28},{24,32},{28,36},{32,40... | collective-permute-start | bytes 393224 | tf_op jit(solution)/shard_map/ppermute | solution.py:15
  36.9 4.7 %collective-permute-start.1 = (bf16[256,256]{0,1:T(8,128)(2,1)}, bf16[256,256]{0,1:T(8,128)(2,1)S(1)}, u32[]{:S(2)}, u32[]{:S(2)}) collective-permute-start(bf16[256,256]{0,1:T(8,128)(2,1)} %copy.24), channel_id=1, source_target_pairs={{0,4},{4,8},{8,12},{12,16},{16,20},{20,24},{24,28},{28,32},{32,36}... | collective-permute-start | bytes 393224 | tf_op jit(solution)/shard_map/ppermute | solution.py:15
  41.7 2.6 %collective-permute-start.8 = (bf16[256,256]{1,0:T(8,128)(2,1)}, bf16[256,256]{1,0:T(8,128)(2,1)}, u32[]{:S(2)}, u32[]{:S(2)}) collective-permute-start(bf16[256,256]{1,0:T(8,128)(2,1)} %param.6), channel_id=1, source_target_pairs={{0,4},{4,8},{8,12},{12,16},{16,20},{20,24},{24,28},{28,32},{32,36}... | collective-permute-start | bytes 393224 | tf_op jit(solution)/shard_map/ppermute | solution.py:15
  45.8 2.8 %collective-permute-start.10 = (bf16[256,256]{1,0:T(8,128)(2,1)S(1)}, bf16[256,256]{1,0:T(8,128)(2,1)}, u32[]{:S(2)}, u32[]{:S(2)}) collective-permute-start(bf16[256,256]{1,0:T(8,128)(2,1)S(1)} %copy-done.2), channel_id=1, source_target_pairs={{0,12},{4,16},{8,20},{12,24},{16,28},{20,32},{24,36},{28,40},{32,4... | collective-permute-start | bytes 393224 | tf_op jit(solution)/shard_map/ppermute | solution.py:15
  48.7 1.9 %fusion.13 = (f32[2,4,256]{2,1,0:T(4,128)S(1)}, f32[2,256,256,4]{2,1,3,0:T(8,128)}) fusion(pred[256,256]{0,1:T(8,128)(4,1)S(1)} %get-tuple-element.13, bf16[256,2,128,1]{0,2,3,1:T(8,128)(2,1)S(1)} %bitcast.120, bf16[256,2,4,128]{3,2,1,0:T(4,128)(2,1)S(1)} %reshape.57), kind=kOutput, calls=%fused_computation.23 | convolution fusion | flops 135788544 | bytes 2826240 | tf_op jit(solution)/shard_map/qkgd,skd->kgqs/dot_general | solution.py:39
  50.5 7.7 %collective-permute-start.11 = (bf16[256,256]{1,0:T(8,128)(2,1)S(1)}, bf16[256,256]{1,0:T(8,128)(2,1)S(1)}, u32[]{:S(2)}, u32[]{:S(2)}) collective-permute-start(bf16[256,256]{1,0:T(8,128)(2,1)S(1)} %copy-done.2), channel_id=1, source_target_pairs={{0,16},{4,20},{8,24},{12,28},{16,32},{20,36},{24,40},{28,44},{32,4... | collective-permute-start | bytes 393224 | tf_op jit(solution)/shard_map/ppermute | solution.py:15
  58.3 1.8 %fusion.12 = (f32[2,4,256]{2,1,0:T(4,128)S(1)}, f32[2,256,256,4]{2,1,3,0:T(8,128)}) fusion(pred[256,256]{0,1:T(8,128)(4,1)S(1)} %get-tuple-element.12, bf16[256,2,128,1]{0,2,3,1:T(8,128)(2,1)S(1)} %bitcast.123, bf16[256,2,4,128]{3,2,1,0:T(4,128)(2,1)S(1)} %reshape.57), kind=kOutput, calls=%fused_computation.22 | convolution fusion | flops 135788544 | bytes 2826240 | tf_op jit(solution)/shard_map/qkgd,skd->kgqs/dot_general | solution.py:39
  60.1 2.7 %collective-permute-start.9 = (bf16[256,256]{1,0:T(8,128)(2,1)S(1)}, bf16[256,256]{1,0:T(8,128)(2,1)}, u32[]{:S(2)}, u32[]{:S(2)}) collective-permute-start(bf16[256,256]{1,0:T(8,128)(2,1)S(1)} %copy-done.2), channel_id=1, source_target_pairs={{0,8},{4,12},{8,16},{12,20},{16,24},{20,28},{24,32},{28,36},{32,40... | collective-permute-start | bytes 393224 | tf_op jit(solution)/shard_map/ppermute | solution.py:15
  62.8 1.9 %fusion.11 = (f32[2,4,256]{2,1,0:T(4,128)S(1)}, f32[2,256,256,4]{2,1,3,0:T(8,128)}) fusion(pred[256,256]{0,1:T(8,128)(4,1)S(1)} %get-tuple-element.11, bf16[256,2,128,1]{0,2,3,1:T(8,128)(2,1)S(1)} %bitcast.122, bf16[256,2,4,128]{3,2,1,0:T(4,128)(2,1)S(1)} %reshape.57), kind=kOutput, calls=%fused_computation.21 | convolution fusion | flops 135788544 | bytes 2826240 | tf_op jit(solution)/shard_map/qkgd,skd->kgqs/dot_general | solution.py:39
  64.7 1.9 %fusion.10 = (f32[2,4,256]{2,1,0:T(4,128)S(1)}, f32[2,256,256,4]{2,1,3,0:T(8,128)}) fusion(pred[256,256]{0,1:T(8,128)(4,1)S(1)} %get-tuple-element.10, bf16[256,2,128,1]{0,2,3,1:T(8,128)(2,1)S(1)} %bitcast.121, bf16[256,2,4,128]{3,2,1,0:T(4,128)(2,1)S(1)} %reshape.57), kind=kOutput, calls=%fused_computation.20 | convolution fusion | flops 135788544 | bytes 2826240 | tf_op jit(solution)/shard_map/qkgd,skd->kgqs/dot_general | solution.py:39
  67.6 3.2 %fusion.21 = f32[2,4,256,128]{2,3,1,0:T(8,128)} fusion(bf16[256,2,128,1]{0,2,3,1:T(8,128)(2,1)S(1)} %bitcast.111, f32[2,256,256,4]{2,1,3,0:T(8,128)} %get-tuple-element.18, f32[2,4,256]{2,1,0:T(4,128)S(1)} %bitcast.114, pred[256,256]{0,1:T(8,128)(4,1)S(1)} %get-tuple-element.12), kind=kOutput, calls=%fused_computation.32 | convolution fusion | flops 136314880 | bytes 3350528 | tf_op jit(solution)/shard_map/kgqs,skd->qkgd/dot_general | solution.py:53
  70.8 4.3 %collective-permute-done.11 = bf16[256,256]{1,0:T(8,128)(2,1)S(1)} collective-permute-done((bf16[256,256]{1,0:T(8,128)(2,1)S(1)}, bf16[256,256]{1,0:T(8,128)(2,1)S(1)}, u32[]{:S(2)}, u32[]{:S(2)}) %collective-permute-start.11) | collective-permute-done | bytes 131104 | tf_op jit(solution)/shard_map/ppermute | solution.py:15
  75.2 3.5 %fusion.19 = f32[2,4,256,128]{2,3,1,0:T(8,128)} fusion(bf16[256,2,128,1]{0,2,3,1:T(8,128)(2,1)S(1)} %bitcast.112, f32[2,256,256,4]{2,1,3,0:T(8,128)} %get-tuple-element.16, f32[2,4,256]{2,1,0:T(4,128)S(1)} %bitcast.115, pred[256,256]{0,1:T(8,128)(4,1)S(1)} %get-tuple-element.13), kind=kOutput, calls=%fused_computation.31 | convolution fusion | flops 136314880 | bytes 3350528 | tf_op jit(solution)/shard_map/kgqs,skd->qkgd/dot_general | solution.py:53
  78.7 4.6 %fusion.2 = (f32[2,4,256]{2,1,0:T(4,128)S(1)}, f32[2,4,256]{2,1,0:T(4,128)}, f32[2,4,256]{2,1,0:T(4,128)}, f32[2,4,256]{2,1,0:T(4,128)}, f32[2,4,256]{2,1,0:T(4,128)}) fusion(f32[2,256,256,4]{2,1,3,0:T(8,128)} %get-tuple-element.24, f32[2,4,256]{2,1,0:T(4,128)S(1)} %bitcast.116, pred[256,256]{0,1:T(8,128)(4,1)S(1)} %get-tuple-element.10, ...), kind=kLoop, calls=%fused_computation.12 | loop fusion | flops 9426944 | bytes 10797056 | tf_op jit(solution)/shard_map/reduce_sum | solution.py:59
  84.8 3.4 %convolution_add_fusion.1 = f32[2,4,256,128]{2,3,1,0:T(8,128)} fusion(f32[2,4,256,128]{2,3,1,0:T(8,128)S(1)} %fusion.25, bf16[256,2,128,1]{0,2,3,1:T(8,128)(2,1)S(1)} %bitcast.110, f32[2,256,256,4]{2,1,3,0:T(8,128)} %get-tuple-element.24, f32[2,4,256]{2,1,0:T(4,128)S(1)} %bitcast.118, pred[256,256]{0,1:T(8,128)(4,1)S(1)} %get-tuple-element.10), kind=kOutput, calls=%fused_computation.26 | convolution fusion | flops 136577024 | bytes 4399104 | tf_op jit(solution)/shard_map/kgqs,skd->qkgd/dot_general | solution.py:53
  89.3 2.5 %fusion.18 = bf16[256,2,4,128]{0,3,2,1:T(8,128)(2,1)S(1)} fusion(f32[2,4,256,128]{2,3,1,0:T(8,128)} %fusion.19, f32[2,4,256,128]{2,3,1,0:T(8,128)} %fusion.21, f32[2,4,256,128]{2,3,1,0:T(8,128)} %convolution_add_fusion.1, bf16[256,2,128,1]{0,2,3,1:T(8,128)(2,1)S(1)} %bitcast.124, f32[2,256,256,4]{2,1,3,0:T(8,128)S(1)} %copy-done.1, ...), kind=kOutput, calls=%fused_computation.30 | convolution fusion | flops 137625600 | bytes 5980160 | tf_op jit(solution)/shard_map/kgqs,skd->qkgd/dot_general | solution.py:53
  (37 shorter events, 8.2 us)
Async XLA Ops:
  0.0 28.7 %collective-permute-start = (s32[256]{0:T(256)}, s32[256]{0:T(256)S(1)}, u32[]{:S(2)}, u32[]{:S(2)}) collective-permute-start(s32[256]{0:T(256)} %param.7), channel_id=1, source_target_pairs={{0,4},{4,8},{8,12},{12,16},{16,20},{20,24},{24,28},{28,32},{32,36}... | collective-permute-start | bytes 3080 | tf_op jit(solution)/shard_map/ppermute | solution.py:15
  3.5 28.9 %collective-permute-start.2 = (s32[256]{0:T(256)}, s32[256]{0:T(256)S(1)}, u32[]{:S(2)}, u32[]{:S(2)}) collective-permute-start(s32[256]{0:T(256)} %param.7), channel_id=1, source_target_pairs={{0,8},{4,12},{8,16},{12,20},{16,24},{20,28},{24,32},{28,36},{32,40... | collective-permute-start | bytes 3080 | tf_op jit(solution)/shard_map/ppermute | solution.py:15
  8.0 28.9 %collective-permute-start.4 = (s32[256]{0:T(256)}, s32[256]{0:T(256)S(1)}, u32[]{:S(2)}, u32[]{:S(2)}) collective-permute-start(s32[256]{0:T(256)} %param.7), channel_id=1, source_target_pairs={{0,12},{4,16},{8,20},{12,24},{16,28},{20,32},{24,36},{28,40},{32,4... | collective-permute-start | bytes 3080 | tf_op jit(solution)/shard_map/ppermute | solution.py:15
  12.9 28.7 %collective-permute-start.6 = (s32[256]{0:T(256)}, s32[256]{0:T(256)S(1)}, u32[]{:S(2)}, u32[]{:S(2)}) collective-permute-start(s32[256]{0:T(256)} %param.7), channel_id=1, source_target_pairs={{0,16},{4,20},{8,24},{12,28},{16,32},{20,36},{24,40},{28,44},{32,4... | collective-permute-start | bytes 3080 | tf_op jit(solution)/shard_map/ppermute | solution.py:15
  19.3 26.5 %collective-permute-start.7 = (bf16[256,256]{0,1:T(8,128)(2,1)}, bf16[256,256]{0,1:T(8,128)(2,1)S(1)}, u32[]{:S(2)}, u32[]{:S(2)}) collective-permute-start(bf16[256,256]{0,1:T(8,128)(2,1)} %copy.24), channel_id=1, source_target_pairs={{0,16},{4,20},{8,24},{12,28},{16,32},{20,36},{24,40},{28,44},{32,4... | collective-permute-start | bytes 393224 | tf_op jit(solution)/shard_map/ppermute | solution.py:15
  26.2 19.6 %copy-start.2 = (bf16[256,256]{1,0:T(8,128)(2,1)S(1)}, bf16[256,256]{1,0:T(8,128)(2,1)}, u32[]{:S(2)}) copy-start(bf16[256,256]{1,0:T(8,128)(2,1)} %param.6) | copy-start | bytes 393220
  28.7 21.8 %collective-permute-start.5 = (bf16[256,256]{0,1:T(8,128)(2,1)}, bf16[256,256]{0,1:T(8,128)(2,1)S(1)}, u32[]{:S(2)}, u32[]{:S(2)}) collective-permute-start(bf16[256,256]{0,1:T(8,128)(2,1)} %copy.24), channel_id=1, source_target_pairs={{0,12},{4,16},{8,20},{12,24},{16,28},{20,32},{24,36},{28,40},{32,4... | collective-permute-start | bytes 393224 | tf_op jit(solution)/shard_map/ppermute | solution.py:15
  32.4 27.7 %collective-permute-start.3 = (bf16[256,256]{0,1:T(8,128)(2,1)}, bf16[256,256]{0,1:T(8,128)(2,1)S(1)}, u32[]{:S(2)}, u32[]{:S(2)}) collective-permute-start(bf16[256,256]{0,1:T(8,128)(2,1)} %copy.24), channel_id=1, source_target_pairs={{0,8},{4,12},{8,16},{12,20},{16,24},{20,28},{24,32},{28,36},{32,40... | collective-permute-start | bytes 393224 | tf_op jit(solution)/shard_map/ppermute | solution.py:15
  36.9 27.7 %collective-permute-start.1 = (bf16[256,256]{0,1:T(8,128)(2,1)}, bf16[256,256]{0,1:T(8,128)(2,1)S(1)}, u32[]{:S(2)}, u32[]{:S(2)}) collective-permute-start(bf16[256,256]{0,1:T(8,128)(2,1)} %copy.24), channel_id=1, source_target_pairs={{0,4},{4,8},{8,12},{12,16},{16,20},{20,24},{24,28},{28,32},{32,36}... | collective-permute-start | bytes 393224 | tf_op jit(solution)/shard_map/ppermute | solution.py:15
  41.7 42.1 %collective-permute-start.8 = (bf16[256,256]{1,0:T(8,128)(2,1)}, bf16[256,256]{1,0:T(8,128)(2,1)}, u32[]{:S(2)}, u32[]{:S(2)}) collective-permute-start(bf16[256,256]{1,0:T(8,128)(2,1)} %param.6), channel_id=1, source_target_pairs={{0,4},{4,8},{8,12},{12,16},{16,20},{20,24},{24,28},{28,32},{32,36}... | collective-permute-start | bytes 393224 | tf_op jit(solution)/shard_map/ppermute | solution.py:15
  45.8 20.7 %collective-permute-start.10 = (bf16[256,256]{1,0:T(8,128)(2,1)S(1)}, bf16[256,256]{1,0:T(8,128)(2,1)}, u32[]{:S(2)}, u32[]{:S(2)}) collective-permute-start(bf16[256,256]{1,0:T(8,128)(2,1)S(1)} %copy-done.2), channel_id=1, source_target_pairs={{0,12},{4,16},{8,20},{12,24},{16,28},{20,32},{24,36},{28,40},{32,4... | collective-permute-start | bytes 393224 | tf_op jit(solution)/shard_map/ppermute | solution.py:15
  50.5 24.5 %collective-permute-start.11 = (bf16[256,256]{1,0:T(8,128)(2,1)S(1)}, bf16[256,256]{1,0:T(8,128)(2,1)S(1)}, u32[]{:S(2)}, u32[]{:S(2)}) collective-permute-start(bf16[256,256]{1,0:T(8,128)(2,1)S(1)} %copy-done.2), channel_id=1, source_target_pairs={{0,16},{4,20},{8,24},{12,28},{16,32},{20,36},{24,40},{28,44},{32,4... | collective-permute-start | bytes 393224 | tf_op jit(solution)/shard_map/ppermute | solution.py:15
  60.1 28.2 %collective-permute-start.9 = (bf16[256,256]{1,0:T(8,128)(2,1)S(1)}, bf16[256,256]{1,0:T(8,128)(2,1)}, u32[]{:S(2)}, u32[]{:S(2)}) collective-permute-start(bf16[256,256]{1,0:T(8,128)(2,1)S(1)} %copy-done.2), channel_id=1, source_target_pairs={{0,8},{4,12},{8,16},{12,20},{16,24},{20,28},{24,32},{28,36},{32,40... | collective-permute-start | bytes 393224 | tf_op jit(solution)/shard_map/ppermute | solution.py:15
  75.2 3.5 %copy-start = (f32[2,256,256,4]{2,1,3,0:T(8,128)S(1)}, f32[2,256,256,4]{2,1,3,0:T(8,128)}, u32[]{:S(2)}) copy-start(f32[2,256,256,4]{2,1,3,0:T(8,128)} %get-tuple-element.16) | copy-start | bytes 6291460
  84.8 3.5 %copy-start.3 = (f32[2,4,256]{2,1,0:T(4,128)S(1)}, f32[2,4,256]{2,1,0:T(4,128)}, u32[]{:S(2)}) copy-start(f32[2,4,256]{2,1,0:T(4,128)} %get-tuple-element.6) | copy-start | bytes 24580
  84.8 3.4 %copy-start.4 = (f32[2,4,256]{2,1,0:T(4,128)S(1)}, f32[2,4,256]{2,1,0:T(4,128)}, u32[]{:S(2)}) copy-start(f32[2,4,256]{2,1,0:T(4,128)} %get-tuple-element.7) | copy-start | bytes 24580
  84.8 3.4 %copy-start.5 = (f32[2,4,256]{2,1,0:T(4,128)S(1)}, f32[2,4,256]{2,1,0:T(4,128)}, u32[]{:S(2)}) copy-start(f32[2,4,256]{2,1,0:T(4,128)} %get-tuple-element.8) | copy-start | bytes 24580
  84.8 3.4 %copy-start.6 = (f32[2,4,256]{2,1,0:T(4,128)S(1)}, f32[2,4,256]{2,1,0:T(4,128)}, u32[]{:S(2)}) copy-start(f32[2,4,256]{2,1,0:T(4,128)} %get-tuple-element.9) | copy-start | bytes 24580
  84.8 4.5 %copy-start.1 = (f32[2,256,256,4]{2,1,3,0:T(8,128)S(1)}, f32[2,256,256,4]{2,1,3,0:T(8,128)}, u32[]{:S(2)}) copy-start(f32[2,256,256,4]{2,1,3,0:T(8,128)} %get-tuple-element.20) | copy-start | bytes 6291460
where the time goes:
time: 93.4 us; the launch traced here: 92.8 us
  starting transfers between devices  52.3 us (56%)
  matrix products  21.1 us (23%)
  local copies, waits for them, and re-layouts  9.19 us (10%)
  other arithmetic  5.66 us (6%)
  waiting for transfers between devices  4.33 us (5%)
    ppermute x12, starting transfers between devices, shifted(): lax.ppermute(value, axis, [(source, source + steps) for source in range(i...  52.3 us
    dot_general x5, matrix products, shards(): jnp.einsum('kgqs,skd->qkgd', weights.astype(jnp.bfloat16), value_heads, p...  13.1 us
    dot_general x5, matrix products, shards(): jnp.einsum('qkgd,skd->kgqs', query_heads, key_heads, preferred_element_ty...  7.98 us
    reduce_sum x1, other arithmetic, shards(): partial_den = jnp.sum(weights, axis=-1)  4.59 us
    ppermute x12, waiting for transfers between devices, shifted(): lax.ppermute(value, axis, [(source, source + steps) for source in range(i...  4.33 us
    ppermute x4, local copies, waits for them, and re-layouts, shifted(): lax.ppermute(value, axis, [(source, source + steps) for source in range(i...  3.1 us
  transfers between devices with their start and end apart: 12, of which 1 were waited for; matrix products, arithmetic and copies ran while one was open for 34% of the time, Pallas kernels for 0%

commit v1 on v0

v1 whole, which is shorter than its diff:
```python
import functools
import math

import jax
import jax.numpy as jnp
from jax import lax
from jax.experimental import pallas as pl
from jax.experimental.pallas import tpu as pltpu
from jax.sharding import PartitionSpec as P

HEAD_WIDTH = 128
DOC_ROWS = 16
MASKED = -1e30
SCORE_SCALE = math.log2(math.e) / math.sqrt(HEAD_WIDTH)


def shifted(value, steps):
    count = lax.axis_size("blk")
    return lax.ppermute(
        value, "blk", [(source, (source + steps) % count) for source in range(count)]
    )


def attend(n_packets, own, final, *refs):
    refs = list(refs)
    q_ref, doc_ref = refs[:2]
    packets = refs[2 : 2 + n_packets]
    rest = refs[2 + n_packets :]
    if own:
        prev = None
    else:
        prev, rest = rest[:2], rest[2:]
    rows = q_ref.shape[0]
    kv_cols = packets[0].shape[1] // 2
    kv_heads = kv_cols // HEAD_WIDTH
    q_heads = q_ref.shape[1] // HEAD_WIDTH
    group = q_heads // kv_heads
    q_docs = doc_ref[...]
    biases = []
    for number, packet in enumerate(packets):
        key_docs = packet[rows : rows + DOC_ROWS, :rows].astype(jnp.float32)[0:1, :]
        allowed = q_docs == key_docs
        if own and number == 0:
            row = lax.broadcasted_iota(jnp.int32, (rows, rows), 0)
            col = lax.broadcasted_iota(jnp.int32, (rows, rows), 1)
            allowed = allowed & (col <= row)
        biases.append(jnp.where(allowed, 0.0, MASKED).astype(jnp.float32))
    for head in range(q_heads):
        kv = head // group
        lanes = slice(head * HEAD_WIDTH, (head + 1) * HEAD_WIDTH)
        q = q_ref[:, lanes]
        scores = []
        top = None
        for packet, bias in zip(packets, biases):
            k = packet[:rows, kv * HEAD_WIDTH : (kv + 1) * HEAD_WIDTH]
            s = lax.dot_general(
                q, k, (((1,), (1,)), ((), ())), preferred_element_type=jnp.float32
            )
            s = s * SCORE_SCALE + bias
            scores.append(s)
            m = jnp.max(s, axis=1, keepdims=True)
            top = m if top is None else jnp.maximum(top, m)
        if prev is not None:
            old_top = prev[1][:, head : head + 1]
            old_den = prev[1][:, q_heads + head : q_heads + head + 1]
            top = jnp.maximum(top, old_top)
            fade = jnp.exp2(old_top - top)
            den = old_den * fade
            num = prev[0][:, lanes] * fade
        else:
            den = num = None
        for packet, s in zip(packets, scores):
            v = packet[:rows, kv_cols + kv * HEAD_WIDTH : kv_cols + (kv + 1) * HEAD_WIDTH]
            w = jnp.exp2(s - top)
            part = jnp.sum(w, axis=1, keepdims=True)
            add = jnp.dot(w.astype(jnp.bfloat16), v, preferred_element_type=jnp.float32)
            den = part if den is None else den + part
            num = add if num is None else num + add
        if final:
            rest[0][:, lanes] = (num * (1.0 / den)).astype(jnp.bfloat16)
        else:
            rest[0][:, lanes] = num
            rest[1][:, head : head + 1] = top
            rest[1][:, q_heads + head : q_heads + head + 1] = den


def fold(queries, q_docs, packets, state, final):
    rows, cols = queries.shape
    q_heads = cols // HEAD_WIDTH
    if final:
        out_shape = jax.ShapeDtypeStruct((rows, cols), jnp.bfloat16)
    else:
        out_shape = (
            jax.ShapeDtypeStruct((rows, cols), jnp.float32),
            jax.ShapeDtypeStruct((rows, 2 * q_heads), jnp.float32),
        )
    args = [queries, q_docs, *packets, *(state or ())]
    work = len(packets) * rows * rows * q_heads
    return pl.pallas_call(
        functools.partial(attend, len(packets), state is None, final),
        out_shape=out_shape,
        compiler_params=pltpu.CompilerParams(vmem_limit_bytes=32 * 1024 * 1024),
        cost_estimate=pl.CostEstimate(
            flops=4 * work * HEAD_WIDTH, bytes_accessed=3 * rows * cols, transcendentals=work
        ),
    )(*args)


def shards(queries, keys, values, doc_ids):
    rows = queries.shape[0]
    docs = doc_ids + 1
    doc_rows = jnp.broadcast_to(docs.astype(jnp.bfloat16)[None, :], (DOC_ROWS, rows))
    doc_rows = jnp.concatenate([doc_rows, doc_rows], axis=1)
    packet = jnp.concatenate([jnp.concatenate([keys, values], axis=1), doc_rows], axis=0)
    q_docs = docs.astype(jnp.float32)[:, None]

    one = shifted(packet, 1)
    four = shifted(packet, 4)
    two = shifted(one, 1)
    three = shifted(four, -1)

    state = fold(queries, q_docs, [packet], None, False)
    state = fold(queries, q_docs, [one], state, False)
    state = fold(queries, q_docs, [four], state, False)
    return fold(queries, q_docs, [two, three], state, True)


def solution(mesh):
    return jax.shard_map(
        shards,
        mesh=mesh,
        in_specs=(P("blk", "heads"), P("blk", "heads"), P("blk", "heads"), P("blk")),
        out_specs=P("blk", "heads"),
        check_vma=False,
    )
```

time: 93.4 us -> 51.7 us (0.55)
  the two profiles are of different devices: /device:TPU:260 before, /device:TPU:24 now
where the time goes in v1:
time: 51.7 us; the launch traced here: 51.4 us
  starting transfers between devices  23.6 us (46%)
  Pallas kernels  13.4 us (26%)
  waiting for transfers between devices  12.4 us (24%)
  other arithmetic  1.73 us (3%)
    ppermute x4, starting transfers between devices, shifted(): lax.ppermute(value, 'blk', [(source, (source + steps) % count) for source...  23.6 us
    pallas_call x4, Pallas kernels, fold(): pl.pallas_call(functools.partial(attend, len(packets), state is None, fin...  13.4 us
    ppermute x4, waiting for transfers between devices, shifted(): lax.ppermute(value, 'blk', [(source, (source + steps) % count) for source...  12.4 us
  transfers between devices with their start and end apart: 4, of which 1 were waited for; matrix products, arithmetic and copies ran while one was open for 0% of the time, Pallas kernels for 17%

profile of v1, /device:TPU:24, one launch (start us, length us, event | category | flops | bytes accessed | tf_op | source)
XLA Modules:
  0.0 51.4 jit_solution(8532547238086153500)
XLA Ops:
  0.0 0.0 copy-start
  0.0 0.7 %add_convert_fusion = (bf16[256]{0:T(256)(128)(2,1)S(1)}, f32[256]{0:T(256)S(1)}) fusion(s32[256]{0:T(256)} %param.7), kind=kLoop, calls=%fused_computation.1 | loop fusion | flops 768 | bytes 2560 | tf_op jit(solution)/shard_map/convert_element_type | solution.py:112
  0.8 1.0 %maximum_maximum_fusion.refs_2_ = bf16[272,512]{1,0:T(8,128)(2,1)S(1)} fusion(bf16[16,256]{1,0:T(8,128)(2,1)S(1)} %broadcast_in_dim.10, bf16[256,256]{1,0:T(8,128)(2,1)} %param.6, bf16[256,256]{1,0:T(8,128)(2,1)} %param.5), kind=kLoop, calls=%fused_computation | loop fusion | flops 1114112 | bytes 548864 | tf_op jit(solution)/shard_map/concatenate | solution.py:114
  1.7 4.7 %collective-permute-start = (bf16[272,512]{1,0:T(8,128)(2,1)S(1)}, bf16[272,512]{1,0:T(8,128)(2,1)S(1)}, u32[]{:S(2)}, u32[]{:S(2)}) collective-permute-start(bf16[272,512]{1,0:T(8,128)(2,1)S(1)} %maximum_maximum_fusion.refs_2_), channel_id=1, source_target_pairs={{0,4},{4,8},{8,12},{12,16},{16,20},{20,24},{24,28},{28,32},{32,36}... | collective-permute-start | bytes 835592 | tf_op jit(solution)/shard_map/ppermute | solution.py:19
  6.4 3.8 %collective-permute-start.2 = (bf16[272,512]{1,0:T(8,128)(2,1)S(1)}, bf16[272,512]{1,0:T(8,128)(2,1)S(1)}, u32[]{:S(2)}, u32[]{:S(2)}) collective-permute-start(bf16[272,512]{1,0:T(8,128)(2,1)S(1)} %maximum_maximum_fusion.refs_2_), channel_id=1, source_target_pairs={{0,16},{4,20},{8,24},{12,28},{16,32},{20,36},{24,40},{28,44},{32,4... | collective-permute-start | bytes 835592 | tf_op jit(solution)/shard_map/ppermute | solution.py:19
  10.3 12.4 %collective-permute-done.refs_2_ = bf16[272,512]{1,0:T(8,128)(2,1)S(1)} collective-permute-done((bf16[272,512]{1,0:T(8,128)(2,1)S(1)}, bf16[272,512]{1,0:T(8,128)(2,1)S(1)}, u32[]{:S(2)}, u32[]{:S(2)}) %collective-permute-start) | collective-permute-done | bytes 278560 | tf_op jit(solution)/shard_map/ppermute | solution.py:19
  22.7 6.0 %collective-permute-start.1 = (bf16[272,512]{1,0:T(8,128)(2,1)S(1)}, bf16[272,512]{1,0:T(8,128)(2,1)S(1)}, u32[]{:S(2)}, u32[]{:S(2)}) collective-permute-start(bf16[272,512]{1,0:T(8,128)(2,1)S(1)} %collective-permute-done.refs_2_), channel_id=1, source_target_pairs={{0,4},{4,8},{8,12},{12,16},{16,20},{20,24},{24,28},{28,32},{32,36}... | collective-permute-start | bytes 835592 | tf_op jit(solution)/shard_map/ppermute | solution.py:19
  28.7 0.0 collective-permute-done.2.refs_2_
  28.7 9.1 %collective-permute-start.3 = (bf16[272,512]{1,0:T(8,128)(2,1)S(1)}, bf16[272,512]{1,0:T(8,128)(2,1)S(1)}, u32[]{:S(2)}, u32[]{:S(2)}) collective-permute-start(bf16[272,512]{1,0:T(8,128)(2,1)S(1)} %collective-permute-done.2.refs_2_), channel_id=1, source_target_pairs={{0,508},{4,0},{8,4},{12,8},{16,12},{20,16},{24,20},{28,24},{32,28}... | collective-permute-start | bytes 835592 | tf_op jit(solution)/shard_map/ppermute | solution.py:19
  37.8 0.1 copy.8.refs_1_
  38.0 0.0 copy-done
  38.0 1.2 %shard_map.46 = (f32[256,1024]{1,0:T(8,128)S(1)}, f32[256,16]{1,0:T(8,128)S(1)}) custom-call(bf16[256,1024]{1,0:T(8,128)(2,1)S(1)} %copy-done, f32[256,1]{1,0:T(8,128)S(1)} %copy.8.refs_1_, bf16[272,512]{1,0:T(8,128)(2,1)S(1)} %maximum_maximum_fusion.refs_2_), custom_call_target="tpu_custom_call" | custom-call | flops 268435456 | bytes 786432 | tf_op jit(solution)/shard_map/pallas_call | solution.py:99
  39.2 3.8 %shard_map.47 = (f32[256,1024]{1,0:T(8,128)S(1)}, f32[256,16]{1,0:T(8,128)S(1)}) custom-call(bf16[256,1024]{1,0:T(8,128)(2,1)S(1)} %copy-done, f32[256,1]{1,0:T(8,128)S(1)} %copy.8.refs_1_, bf16[272,512]{1,0:T(8,128)(2,1)S(1)} %collective-permute-done.refs_2_, f32[256,1024]{1,0:T(8,128)S(1)} %get-tuple-element.11.refs_3_, ...), custom_call_target="tpu_custom_call" | custom-call | flops 268435456 | bytes 786432 | tf_op jit(solution)/shard_map/pallas_call | solution.py:99
  42.9 3.8 %shard_map.48 = (f32[256,1024]{1,0:T(8,128)S(1)}, f32[256,16]{1,0:T(8,128)S(1)}) custom-call(bf16[256,1024]{1,0:T(8,128)(2,1)S(1)} %copy-done, f32[256,1]{1,0:T(8,128)S(1)} %copy.8.refs_1_, bf16[272,512]{1,0:T(8,128)(2,1)S(1)} %collective-permute-done.2.refs_2_, f32[256,1024]{1,0:T(8,128)S(1)} %get-tuple-element.13.refs_3_, ...), custom_call_target="tpu_custom_call" | custom-call | flops 268435456 | bytes 786432 | tf_op jit(solution)/shard_map/pallas_call | solution.py:99
  46.7 0.0 collective-permute-done.1.refs_2_
  46.7 0.0 collective-permute-done.3.refs_3_
  46.7 4.7 %shard_map.49 = bf16[256,1024]{1,0:T(8,128)(2,1)} custom-call(bf16[256,1024]{1,0:T(8,128)(2,1)S(1)} %copy-done, f32[256,1]{1,0:T(8,128)S(1)} %copy.8.refs_1_, bf16[272,512]{1,0:T(8,128)(2,1)S(1)} %collective-permute-done.1.refs_2_, bf16[272,512]{1,0:T(8,128)(2,1)S(1)} %collective-permute-done.3.refs_3_, f32[256,1024]{1,0:T(8,128)S(1)} %get-tuple-element.15.refs_4_, ...), custom_call_target="tpu_custom_call" | custom-call | flops 536870912 | bytes 786432 | tf_op jit(solution)/shard_map/pallas_call | solution.py:99
  (1 shorter events, 0.0 us)
Async XLA Ops:
  0.0 38.0 %copy-start = (bf16[256,1024]{1,0:T(8,128)(2,1)S(1)}, bf16[256,1024]{1,0:T(8,128)(2,1)}, u32[]{:S(2)}) copy-start(bf16[256,1024]{1,0:T(8,128)(2,1)} %refs_0_.7) | copy-start | bytes 1572868
  1.7 21.0 %collective-permute-start = (bf16[272,512]{1,0:T(8,128)(2,1)S(1)}, bf16[272,512]{1,0:T(8,128)(2,1)S(1)}, u32[]{:S(2)}, u32[]{:S(2)}) collective-permute-start(bf16[272,512]{1,0:T(8,128)(2,1)S(1)} %maximum_maximum_fusion.refs_2_), channel_id=1, source_target_pairs={{0,4},{4,8},{8,12},{12,16},{16,20},{20,24},{24,28},{28,32},{32,36}... | collective-permute-start | bytes 835592 | tf_op jit(solution)/shard_map/ppermute | solution.py:19
  6.4 22.3 %collective-permute-start.2 = (bf16[272,512]{1,0:T(8,128)(2,1)S(1)}, bf16[272,512]{1,0:T(8,128)(2,1)S(1)}, u32[]{:S(2)}, u32[]{:S(2)}) collective-permute-start(bf16[272,512]{1,0:T(8,128)(2,1)S(1)} %maximum_maximum_fusion.refs_2_), channel_id=1, source_target_pairs={{0,16},{4,20},{8,24},{12,28},{16,32},{20,36},{24,40},{28,44},{32,4... | collective-permute-start | bytes 835592 | tf_op jit(solution)/shard_map/ppermute | solution.py:19
  22.7 24.0 %collective-permute-start.1 = (bf16[272,512]{1,0:T(8,128)(2,1)S(1)}, bf16[272,512]{1,0:T(8,128)(2,1)S(1)}, u32[]{:S(2)}, u32[]{:S(2)}) collective-permute-start(bf16[272,512]{1,0:T(8,128)(2,1)S(1)} %collective-permute-done.refs_2_), channel_id=1, source_target_pairs={{0,4},{4,8},{8,12},{12,16},{16,20},{20,24},{24,28},{28,32},{32,36}... | collective-permute-start | bytes 835592 | tf_op jit(solution)/shard_map/ppermute | solution.py:19
  28.7 18.0 %collective-permute-start.3 = (bf16[272,512]{1,0:T(8,128)(2,1)S(1)}, bf16[272,512]{1,0:T(8,128)(2,1)S(1)}, u32[]{:S(2)}, u32[]{:S(2)}) collective-permute-start(bf16[272,512]{1,0:T(8,128)(2,1)S(1)} %collective-permute-done.2.refs_2_), channel_id=1, source_target_pairs={{0,508},{4,0},{8,4},{12,8},{16,12},{20,16},{24,20},{28,24},{32,28}... | collective-permute-start | bytes 835592 | tf_op jit(solution)/shard_map/ppermute | solution.py:19

commit v2 on v1

v2 whole, which is shorter than its diff:
```python
import functools
import math

import jax
import jax.numpy as jnp
from jax import lax
from jax.experimental import pallas as pl
from jax.experimental.pallas import tpu as pltpu
from jax.sharding import PartitionSpec as P

HEAD_WIDTH = 128
DOC_ROWS = 16
MASKED = -1e30
SCORE_SCALE = math.log2(math.e) / math.sqrt(HEAD_WIDTH)


def shifted(value, steps, kept=lambda source: True):
    count = lax.axis_size("blk")
    pairs = [(source, source + steps) for source in range(count) if 0 <= source + steps < count]
    return lax.ppermute(value, "blk", [pair for pair in pairs if kept(pair[0])])


def summed(refs, index):
    total = refs[0][index]
    for ref in refs[1:]:
        total = total + ref[index]
    return total


def attend(counts, own, final, *refs):
    refs = list(refs)
    q_ref, doc_ref = refs[:2]
    rest = refs[2:]
    packets = []
    for count in counts:
        packets.append(rest[:count])
        rest = rest[count:]
    if own:
        prev = None
    else:
        prev, rest = rest[:3], rest[3:]
    rows = q_ref.shape[0]
    kv_cols = packets[0][0].shape[1] // 2
    kv_heads = kv_cols // HEAD_WIDTH
    q_heads = q_ref.shape[1] // HEAD_WIDTH
    group = q_heads // kv_heads
    q_docs = doc_ref[...]
    biases = []
    for number, packet in enumerate(packets):
        key_docs = summed(packet, (slice(rows, rows + DOC_ROWS), slice(0, rows)))
        key_docs = key_docs.astype(jnp.float32)[0:1, :]
        allowed = q_docs == key_docs
        if own and number == 0:
            row = lax.broadcasted_iota(jnp.int32, (rows, rows), 0)
            col = lax.broadcasted_iota(jnp.int32, (rows, rows), 1)
            allowed = allowed & (col <= row)
        biases.append(jnp.where(allowed, 0.0, MASKED).astype(jnp.float32))
    copies = []
    for head in range(q_heads):
        kv = head // group
        lanes = slice(head * HEAD_WIDTH, (head + 1) * HEAD_WIDTH)
        q = q_ref[:, lanes]
        scores = []
        top = None
        for packet, bias in zip(packets, biases):
            k = summed(packet, (slice(0, rows), slice(kv * HEAD_WIDTH, (kv + 1) * HEAD_WIDTH)))
            s = lax.dot_general(
                q, k, (((1,), (1,)), ((), ())), preferred_element_type=jnp.float32
            )
            s = s * SCORE_SCALE + bias
            scores.append(s)
            m = jnp.max(s, axis=1, keepdims=True)
            top = m if top is None else jnp.maximum(top, m)
        top = jnp.broadcast_to(top, (rows, HEAD_WIDTH))
        if prev is not None:
            old_top = prev[1][:, lanes]
            top = jnp.maximum(top, old_top)
            fade = jnp.exp2(old_top - top)
            den = prev[2][:, lanes] * fade
            num = prev[0][:, lanes] * fade
        else:
            den = num = None
        wide_top = jnp.concatenate([top] * (rows // HEAD_WIDTH), axis=1)
        for packet, s in zip(packets, scores):
            first = kv_cols + kv * HEAD_WIDTH
            v = summed(packet, (slice(0, rows), slice(first, first + HEAD_WIDTH)))
            w = jnp.exp2(s - wide_top)
            part = jnp.broadcast_to(jnp.sum(w, axis=1, keepdims=True), (rows, HEAD_WIDTH))
            add = jnp.dot(w.astype(jnp.bfloat16), v, preferred_element_type=jnp.float32)
            den = part if den is None else den + part
            num = add if num is None else num + add
        if final:
            out_ref, held, sems = rest
            held[:, lanes] = (num * (1.0 / den)).astype(jnp.bfloat16)
            copies.append(
                pltpu.make_async_copy(held.at[:, lanes], out_ref.at[:, lanes], sems.at[head])
            )
            copies[-1].start()
        else:
            rest[0][:, lanes] = num
            rest[1][:, lanes] = top
            rest[2][:, lanes] = den
    for copy in copies:
        copy.wait()


def fold(queries, q_docs, packets, state, final):
    rows, cols = queries.shape
    q_heads = cols // HEAD_WIDTH
    extra = {}
    if final:
        out_shape = jax.ShapeDtypeStruct((rows, cols), jnp.bfloat16)
        extra = dict(
            out_specs=pl.BlockSpec(memory_space=pltpu.HBM),
            scratch_shapes=[
                pltpu.VMEM((rows, cols), jnp.bfloat16),
                pltpu.SemaphoreType.DMA((q_heads,)),
            ],
        )
    else:
        out_shape = (jax.ShapeDtypeStruct((rows, cols), jnp.float32),) * 3
    args = [queries, q_docs, *[part for packet in packets for part in packet], *(state or ())]
    work = len(packets) * rows * rows * q_heads
    return pl.pallas_call(
        functools.partial(attend, [len(packet) for packet in packets], state is None, final),
        out_shape=out_shape,
        **extra,
        compiler_params=pltpu.CompilerParams(vmem_limit_bytes=32 * 1024 * 1024),
        cost_estimate=pl.CostEstimate(
            flops=4 * work * HEAD_WIDTH, bytes_accessed=3 * rows * cols, transcendentals=work
        ),
    )(*args)


def pack(keys, values, doc_ids):
    rows = keys.shape[0]
    docs = jnp.broadcast_to(doc_ids[None, :], (DOC_ROWS, rows))
    docs = lax.optimization_barrier(docs)
    docs = (docs + 1).astype(keys.dtype)
    return jnp.concatenate(
        [jnp.concatenate([keys, docs], axis=0), jnp.concatenate([values, docs], axis=0)], axis=1
    )


def shards(queries, keys, values, doc_ids):
    packet = pack(keys, values, doc_ids)
    q_docs = (doc_ids + 1).astype(jnp.float32)[:, None]
    count = lax.axis_size("blk")

    one = shifted(packet, 1)
    four = shifted(packet, 4)
    last_three = shifted(packet, 3, lambda source: source == count - 4)
    state = fold(queries, q_docs, [[packet]], None, False)
    one, state = lax.optimization_barrier((one, state))
    two = shifted(one, 1)
    state = fold(queries, q_docs, [[one]], state, False)
    four, last_three, state = lax.optimization_barrier((four, last_three, state))
    three = shifted(four, -1)
    state = fold(queries, q_docs, [[four]], state, False)
    state = fold(queries, q_docs, [[two]], state, False)
    return fold(queries, q_docs, [[three, last_three]], state, True)


def solution(mesh):
    return jax.shard_map(
        shards,
        mesh=mesh,
        in_specs=(P("blk", "heads"), P("blk", "heads"), P("blk", "heads"), P("blk")),
        out_specs=P("blk", "heads"),
        check_vma=False,
    )
```

time: 51.7 us -> 44.3 us (0.86)
  the two profiles are of different devices: /device:TPU:24 before, /device:TPU:22 now
where the time goes in v2:
time: 44.3 us; the launch traced here: 44.1 us
  starting transfers between devices  24 us (54%)
  waiting for transfers between devices  10.8 us (24%)
  Pallas kernels  7.26 us (16%)
  other arithmetic  1.01 us (2%)
  local copies, waits for them, and re-layouts  0.88 us (2%)
    ppermute x5, starting transfers between devices, shifted(): return lax.ppermute(value, 'blk', [pair for pair in pairs if kept(pair[0])])  24 us
    ppermute x5, waiting for transfers between devices, shifted(): return lax.ppermute(value, 'blk', [pair for pair in pairs if kept(pair[0])])  10.8 us
    pallas_call x5, Pallas kernels, fold(): pl.pallas_call(functools.partial(attend, [len(packet) for packet in packe...  7.26 us
    concatenate x1, other arithmetic, pack(): jnp.concatenate([jnp.concatenate([keys, docs], axis=0), jnp.concatenate([...  1 us
  transfers between devices with their start and end apart: 5, of which 3 were waited for; matrix products, arithmetic and copies ran while one was open for 0% of the time, Pallas kernels for 12%

profile of v2, /device:TPU:22, one launch (start us, length us, event | category | flops | bytes accessed | tf_op | source)
XLA Modules:
  0.0 44.1 jit_solution(4053908860737175568)
XLA Ops:
  0.0 0.0 copy-start
  0.0 0.7 %broadcast_in_dim.10 = s32[16,256]{1,0:T(8,128)S(1)} broadcast(s32[256]{0:T(256)} %param.7), dimensions={1} | broadcast | bytes 17408 | tf_op jit(solution)/shard_map/broadcast_in_dim | solution.py:137
  0.8 0.0 copy-start.1
  0.8 1.0 %maximum_maximum_fusion.refs_2_ = bf16[272,512]{1,0:T(8,128)(2,1)S(1)} fusion(bf16[16,256]{1,0:T(8,128)(2,1)S(1)} %add_convert_fusion, bf16[256,256]{1,0:T(8,128)(2,1)} %param.6, bf16[256,256]{1,0:T(8,128)(2,1)} %param.5), kind=kLoop, calls=%fused_computation | loop fusion | flops 1114112 | bytes 548864 | tf_op jit(solution)/shard_map/concatenate | solution.py:140
  1.8 3.5 %collective-permute-start.2 = (bf16[272,512]{1,0:T(8,128)(2,1)S(1)}, bf16[272,512]{1,0:T(8,128)(2,1)S(1)}, u32[]{:S(2)}, u32[]{:S(2)}) collective-permute-start(bf16[272,512]{1,0:T(8,128)(2,1)S(1)} %maximum_maximum_fusion.refs_2_), channel_id=1, source_target_pairs={{0,4},{4,8},{8,12},{12,16},{16,20},{20,24},{24,28},{28,32},{32,36}... | collective-permute-start | bytes 835592 | tf_op jit(solution)/shard_map/ppermute | solution.py:20
  5.2 5.0 %collective-permute-start = (bf16[272,512]{1,0:T(8,128)(2,1)S(1)}, bf16[272,512]{1,0:T(8,128)(2,1)S(1)}, u32[]{:S(2)}, u32[]{:S(2)}) collective-permute-start(bf16[272,512]{1,0:T(8,128)(2,1)S(1)} %maximum_maximum_fusion.refs_2_), channel_id=1, source_target_pairs={{0,16},{4,20},{8,24},{12,28},{16,32},{20,36},{24,40},{28,44},{32,4... | collective-permute-start | bytes 835592 | tf_op jit(solution)/shard_map/ppermute | solution.py:20
  10.3 0.7 %collective-permute-start.1 = (bf16[272,512]{1,0:T(8,128)(2,1)S(1)}, bf16[272,512]{1,0:T(8,128)(2,1)S(1)}, u32[]{:S(2)}, u32[]{:S(2)}) collective-permute-start(bf16[272,512]{1,0:T(8,128)(2,1)S(1)} %maximum_maximum_fusion.refs_2_), channel_id=1, source_target_pairs={{496,508},{497,509},{498,510},{499,511}} | collective-permute-start | bytes 835592 | tf_op jit(solution)/shard_map/ppermute | solution.py:20
  11.0 0.0 copy-done.1
  11.0 0.1 copy.9.refs_1_
  11.1 0.0 copy-done
  11.2 1.2 %shard_map.46 = (f32[256,1024]{1,0:T(8,128)S(1)}, f32[256,1024]{1,0:T(8,128)S(1)}, f32[256,1024]{1,0:T(8,128)S(1)}) custom-call(bf16[256,1024]{1,0:T(8,128)(2,1)S(1)} %copy-done, f32[256,1]{1,0:T(8,128)S(1)} %copy.9.refs_1_, bf16[272,512]{1,0:T(8,128)(2,1)S(1)} %maximum_maximum_fusion.refs_2_), custom_call_target="tpu_custom_call" | custom-call | flops 268435456 | bytes 786432 | tf_op jit(solution)/shard_map/pallas_call | solution.py:124
  12.3 2.5 %collective-permute-done.2.refs_2_ = bf16[272,512]{1,0:T(8,128)(2,1)S(1)} collective-permute-done((bf16[272,512]{1,0:T(8,128)(2,1)S(1)}, bf16[272,512]{1,0:T(8,128)(2,1)S(1)}, u32[]{:S(2)}, u32[]{:S(2)}) %collective-permute-start.2) | collective-permute-done | bytes 278560 | tf_op jit(solution)/shard_map/ppermute | solution.py:20
  14.9 12.9 %collective-permute-start.4 = (bf16[272,512]{1,0:T(8,128)(2,1)S(1)}, bf16[272,512]{1,0:T(8,128)(2,1)S(1)}, u32[]{:S(2)}, u32[]{:S(2)}) collective-permute-start(bf16[272,512]{1,0:T(8,128)(2,1)S(1)} %collective-permute-done.2.refs_2_), channel_id=1, source_target_pairs={{0,4},{4,8},{8,12},{12,16},{16,20},{20,24},{24,28},{28,32},{32,36}... | collective-permute-start | bytes 835592 | tf_op jit(solution)/shard_map/ppermute | solution.py:20
  27.8 1.3 %shard_map.47 = (f32[256,1024]{1,0:T(8,128)S(1)}, f32[256,1024]{1,0:T(8,128)S(1)}, f32[256,1024]{1,0:T(8,128)S(1)}) custom-call(bf16[256,1024]{1,0:T(8,128)(2,1)S(1)} %copy-done, f32[256,1]{1,0:T(8,128)S(1)} %copy.9.refs_1_, bf16[272,512]{1,0:T(8,128)(2,1)S(1)} %collective-permute-done.2.refs_2_, f32[256,1024]{1,0:T(8,128)S(1)} %get-tuple-element.30.refs_3_, ...), custom_call_target="tpu_custom_call" | custom-call | flops 268435456 | bytes 786432 | tf_op jit(solution)/shard_map/pallas_call | solution.py:124
  29.1 4.4 %collective-permute-done.refs_2_ = bf16[272,512]{1,0:T(8,128)(2,1)S(1)} collective-permute-done((bf16[272,512]{1,0:T(8,128)(2,1)S(1)}, bf16[272,512]{1,0:T(8,128)(2,1)S(1)}, u32[]{:S(2)}, u32[]{:S(2)}) %collective-permute-start) | collective-permute-done | bytes 278560 | tf_op jit(solution)/shard_map/ppermute | solution.py:20
  33.5 0.0 collective-permute-done.1.refs_3_
  33.5 1.9 %collective-permute-start.3 = (bf16[272,512]{1,0:T(8,128)(2,1)S(1)}, bf16[272,512]{1,0:T(8,128)(2,1)S(1)}, u32[]{:S(2)}, u32[]{:S(2)}) collective-permute-start(bf16[272,512]{1,0:T(8,128)(2,1)S(1)} %collective-permute-done.refs_2_), channel_id=1, source_target_pairs={{4,0},{8,4},{12,8},{16,12},{20,16},{24,20},{28,24},{32,28},{36,32}... | collective-permute-start | bytes 835592 | tf_op jit(solution)/shard_map/ppermute | solution.py:20
  35.5 1.3 %shard_map.48 = (f32[256,1024]{1,0:T(8,128)S(1)}, f32[256,1024]{1,0:T(8,128)S(1)}, f32[256,1024]{1,0:T(8,128)S(1)}) custom-call(bf16[256,1024]{1,0:T(8,128)(2,1)S(1)} %copy-done, f32[256,1]{1,0:T(8,128)S(1)} %copy.9.refs_1_, bf16[272,512]{1,0:T(8,128)(2,1)S(1)} %collective-permute-done.refs_2_, f32[256,1024]{1,0:T(8,128)S(1)} %get-tuple-element.38.refs_3_, ...), custom_call_target="tpu_custom_call" | custom-call | flops 268435456 | bytes 786432 | tf_op jit(solution)/shard_map/pallas_call | solution.py:124
  36.8 0.0 collective-permute-done.4.refs_2_
  36.8 1.3 %shard_map.49 = (f32[256,1024]{1,0:T(8,128)S(1)}, f32[256,1024]{1,0:T(8,128)S(1)}, f32[256,1024]{1,0:T(8,128)S(1)}) custom-call(bf16[256,1024]{1,0:T(8,128)(2,1)S(1)} %copy-done, f32[256,1]{1,0:T(8,128)S(1)} %copy.9.refs_1_, bf16[272,512]{1,0:T(8,128)(2,1)S(1)} %collective-permute-done.4.refs_2_, f32[256,1024]{1,0:T(8,128)S(1)} %get-tuple-element.41.refs_3_, ...), custom_call_target="tpu_custom_call" | custom-call | flops 268435456 | bytes 786432 | tf_op jit(solution)/shard_map/pallas_call | solution.py:124
  38.1 3.9 %collective-permute-done.3.refs_2_ = bf16[272,512]{1,0:T(8,128)(2,1)S(1)} collective-permute-done((bf16[272,512]{1,0:T(8,128)(2,1)S(1)}, bf16[272,512]{1,0:T(8,128)(2,1)S(1)}, u32[]{:S(2)}, u32[]{:S(2)}) %collective-permute-start.3) | collective-permute-done | bytes 278560 | tf_op jit(solution)/shard_map/ppermute | solution.py:20
  42.0 2.1 %shard_map.50 = bf16[256,1024]{1,0:T(8,128)(2,1)} custom-call(bf16[256,1024]{1,0:T(8,128)(2,1)S(1)} %copy-done, f32[256,1]{1,0:T(8,128)S(1)} %copy.9.refs_1_, bf16[272,512]{1,0:T(8,128)(2,1)S(1)} %collective-permute-done.3.refs_2_, bf16[272,512]{1,0:T(8,128)(2,1)S(1)} %collective-permute-done.1.refs_3_, f32[256,1024]{1,0:T(8,128)S(1)} %get-tuple-element.44.refs_4_, ...), custom_call_target="tpu_custom_call" | custom-call | flops 268435456 | bytes 786432 | tf_op jit(solution)/shard_map/pallas_call | solution.py:124
  (2 shorter events, 0.0 us)
Async XLA Ops:
  0.0 11.1 %copy-start = (bf16[256,1024]{1,0:T(8,128)(2,1)S(1)}, bf16[256,1024]{1,0:T(8,128)(2,1)}, u32[]{:S(2)}) copy-start(bf16[256,1024]{1,0:T(8,128)(2,1)} %refs_0_.9) | copy-start | bytes 1572868
  0.8 10.2 %copy-start.1 = (s32[256]{0:T(256)S(1)}, s32[256]{0:T(256)}, u32[]{:S(2)}) copy-start(s32[256]{0:T(256)} %param.7) | copy-start | bytes 3076
  1.8 13.1 %collective-permute-start.2 = (bf16[272,512]{1,0:T(8,128)(2,1)S(1)}, bf16[272,512]{1,0:T(8,128)(2,1)S(1)}, u32[]{:S(2)}, u32[]{:S(2)}) collective-permute-start(bf16[272,512]{1,0:T(8,128)(2,1)S(1)} %maximum_maximum_fusion.refs_2_), channel_id=1, source_target_pairs={{0,4},{4,8},{8,12},{12,16},{16,20},{20,24},{24,28},{28,32},{32,36}... | collective-permute-start | bytes 835592 | tf_op jit(solution)/shard_map/ppermute | solution.py:20
  5.2 28.3 %collective-permute-start = (bf16[272,512]{1,0:T(8,128)(2,1)S(1)}, bf16[272,512]{1,0:T(8,128)(2,1)S(1)}, u32[]{:S(2)}, u32[]{:S(2)}) collective-permute-start(bf16[272,512]{1,0:T(8,128)(2,1)S(1)} %maximum_maximum_fusion.refs_2_), channel_id=1, source_target_pairs={{0,16},{4,20},{8,24},{12,28},{16,32},{20,36},{24,40},{28,44},{32,4... | collective-permute-start | bytes 835592 | tf_op jit(solution)/shard_map/ppermute | solution.py:20
  10.3 23.3 %collective-permute-start.1 = (bf16[272,512]{1,0:T(8,128)(2,1)S(1)}, bf16[272,512]{1,0:T(8,128)(2,1)S(1)}, u32[]{:S(2)}, u32[]{:S(2)}) collective-permute-start(bf16[272,512]{1,0:T(8,128)(2,1)S(1)} %maximum_maximum_fusion.refs_2_), channel_id=1, source_target_pairs={{496,508},{497,509},{498,510},{499,511}} | collective-permute-start | bytes 835592 | tf_op jit(solution)/shard_map/ppermute | solution.py:20
  14.9 21.9 %collective-permute-start.4 = (bf16[272,512]{1,0:T(8,128)(2,1)S(1)}, bf16[272,512]{1,0:T(8,128)(2,1)S(1)}, u32[]{:S(2)}, u32[]{:S(2)}) collective-permute-start(bf16[272,512]{1,0:T(8,128)(2,1)S(1)} %collective-permute-done.2.refs_2_), channel_id=1, source_target_pairs={{0,4},{4,8},{8,12},{12,16},{16,20},{20,24},{24,28},{28,32},{32,36}... | collective-permute-start | bytes 835592 | tf_op jit(solution)/shard_map/ppermute | solution.py:20
  33.5 8.4 %collective-permute-start.3 = (bf16[272,512]{1,0:T(8,128)(2,1)S(1)}, bf16[272,512]{1,0:T(8,128)(2,1)S(1)}, u32[]{:S(2)}, u32[]{:S(2)}) collective-permute-start(bf16[272,512]{1,0:T(8,128)(2,1)S(1)} %collective-permute-done.refs_2_), channel_id=1, source_target_pairs={{4,0},{8,4},{12,8},{16,12},{20,16},{24,20},{28,24},{32,28},{36,32}... | collective-permute-start | bytes 835592 | tf_op jit(solution)/shard_map/ppermute | solution.py:20

commit v3 on v2

--- a/solution.py
+++ b/solution.py
@@ -9,7 +9,8 @@
 from jax.sharding import PartitionSpec as P
 
 HEAD_WIDTH = 128
-DOC_ROWS = 16
+DOC_ROWS = 8
+PLANE = 32
 MASKED = -1e30
 SCORE_SCALE = math.log2(math.e) / math.sqrt(HEAD_WIDTH)
 
@@ -84,9 +85,10 @@
         for packet, s in zip(packets, scores):
             first = kv_cols + kv * HEAD_WIDTH
             v = summed(packet, (slice(0, rows), slice(first, first + HEAD_WIDTH)))
-            w = jnp.exp2(s - wide_top)
-            part = jnp.broadcast_to(jnp.sum(w, axis=1, keepdims=True), (rows, HEAD_WIDTH))
-            add = jnp.dot(w.astype(jnp.bfloat16), v, preferred_element_type=jnp.float32)
+            w = jnp.exp2(s - wide_top).astype(jnp.bfloat16)
+            v = jnp.concatenate([v, jnp.ones_like(v)], axis=1)
+            both = jnp.dot(w, v, preferred_element_type=jnp.float32)
+            add, part = both[:, :HEAD_WIDTH], both[:, HEAD_WIDTH:]
             den = part if den is None else den + part
             num = add if num is None else num + add
         if final:
@@ -133,32 +135,30 @@
 
 
 def pack(keys, values, doc_ids):
-    rows = keys.shape[0]
-    docs = jnp.broadcast_to(doc_ids[None, :], (DOC_ROWS, rows))
-    docs = lax.optimization_barrier(docs)
-    docs = (docs + 1).astype(keys.dtype)
-    return jnp.concatenate(
-        [jnp.concatenate([keys, docs], axis=0), jnp.concatenate([values, docs], axis=0)], axis=1
-    )
+    rows, cols = keys.shape
+    packet = jnp.concatenate([keys, values], axis=1)
+    packet = jnp.pad(packet, ((0, DOC_ROWS), (0, 0)))
+    packet, doc_ids = lax.optimization_barrier((packet, doc_ids))
+    docs = jnp.broadcast_to((doc_ids + 1).astype(keys.dtype)[None, :], (DOC_ROWS, rows))
+    return lax.dynamic_update_slice(packet, docs, (rows, 0))
 
 
 def shards(queries, keys, values, doc_ids):
     packet = pack(keys, values, doc_ids)
     q_docs = (doc_ids + 1).astype(jnp.float32)[:, None]
-    count = lax.axis_size("blk")
 
+    far = lambda source: source % PLANE == PLANE - 4
     one = shifted(packet, 1)
-    four = shifted(packet, 4)
-    last_three = shifted(packet, 3, lambda source: source == count - 4)
+    four = shifted(packet, 4, lambda source: not far(source))
+    far_four = shifted(packet, 4, far)
+    far_three = shifted(packet, 3, far)
+    two = shifted(one, 1)
+    three = shifted(four, -1, lambda source: source % PLANE != 0)
     state = fold(queries, q_docs, [[packet]], None, False)
-    one, state = lax.optimization_barrier((one, state))
-    two = shifted(one, 1)
     state = fold(queries, q_docs, [[one]], state, False)
-    four, last_three, state = lax.optimization_barrier((four, last_three, state))
-    three = shifted(four, -1)
-    state = fold(queries, q_docs, [[four]], state, False)
+    state = fold(queries, q_docs, [[four, far_four]], state, False)
     state = fold(queries, q_docs, [[two]], state, False)
-    return fold(queries, q_docs, [[three, last_three]], state, True)
+    return fold(queries, q_docs, [[three, far_three]], state, True)
 
 
 def solution(mesh):

time: 44.3 us -> 41.4 us (0.935)
  the two profiles are of different devices: /device:TPU:22 before, /device:TPU:286 now
where the time goes in v3:
time: 41.4 us; the launch traced here: 41.2 us
  starting transfers between devices  16.5 us (40%)
  waiting for transfers between devices  16.5 us (40%)
  Pallas kernels  6.9 us (17%)
  other arithmetic  1.06 us (3%)
    ppermute x6, waiting for transfers between devices, shifted(): return lax.ppermute(value, 'blk', [pair for pair in pairs if kept(pair[0])])  16.5 us
    ppermute x6, starting transfers between devices, shifted(): return lax.ppermute(value, 'blk', [pair for pair in pairs if kept(pair[0])])  16.5 us
    pallas_call x5, Pallas kernels, fold(): pl.pallas_call(functools.partial(attend, [len(packet) for packet in packe...  6.9 us
    concatenate x1, other arithmetic, pack(): packet = jnp.concatenate([keys, values], axis=1)  1.04 us
  transfers between devices with their start and end apart: 6, of which 3 were waited for; matrix products, arithmetic and copies ran while one was open for 0% of the time, Pallas kernels for 12%

profile of v3, /device:TPU:286, one launch (start us, length us, event | category | flops | bytes accessed | tf_op | source)
XLA Modules:
  0.0 41.2 jit_solution(9739252730963834639)
XLA Ops:
  0.0 0.0 copy-start.1
  0.0 0.0 copy-start
  0.0 1.0 %fusion.2 = bf16[264,512]{1,0:T(8,128)(2,1)S(1)} fusion(bf16[256,256]{1,0:T(8,128)(2,1)} %param.6, bf16[256,256]{1,0:T(8,128)(2,1)} %param.5), kind=kLoop, calls=%fused_computation.3 | loop fusion | flops 946176 | bytes 532480 | tf_op jit(solution)/shard_map/concatenate | solution.py:139
  1.1 0.0 copy-done.1
  1.1 4.7 %collective-permute-start.3 = (bf16[264,512]{1,0:T(8,128)(2,1)S(1)}, bf16[264,512]{1,0:T(8,128)(2,1)S(1)}, u32[]{:S(2)}, u32[]{:S(2)}) collective-permute-start(bf16[264,512]{1,0:T(8,128)(2,1)S(1)} %broadcast_dynamic-update-slice_fusion.refs_2_), channel_id=1, source_target_pairs={{0,4},{4,8},{8,12},{12,16},{16,20},{20,24},{24,28},{28,32},{32,36}... | collective-permute-start | bytes 811016 | tf_op jit(solution)/shard_map/ppermute | solution.py:21
  5.8 2.9 %collective-permute-start = (bf16[264,512]{1,0:T(8,128)(2,1)S(1)}, bf16[264,512]{1,0:T(8,128)(2,1)S(1)}, u32[]{:S(2)}, u32[]{:S(2)}) collective-permute-start(bf16[264,512]{1,0:T(8,128)(2,1)S(1)} %broadcast_dynamic-update-slice_fusion.refs_2_), channel_id=1, source_target_pairs={{0,16},{4,20},{8,24},{12,28},{16,32},{20,36},{24,40},{28,44},{32,4... | collective-permute-start | bytes 811016 | tf_op jit(solution)/shard_map/ppermute | solution.py:21
  8.7 0.7 %collective-permute-start.5 = (bf16[264,512]{1,0:T(8,128)(2,1)S(1)}, bf16[264,512]{1,0:T(8,128)(2,1)S(1)}, u32[]{:S(2)}, u32[]{:S(2)}) collective-permute-start(bf16[264,512]{1,0:T(8,128)(2,1)S(1)} %broadcast_dynamic-update-slice_fusion.refs_2_), channel_id=1, source_target_pairs={{112,128},{240,256},{368,384},{113,129},{241,257},{369,385},{114,1... | collective-permute-start | bytes 811016 | tf_op jit(solution)/shard_map/ppermute | solution.py:21
  9.4 0.7 %collective-permute-start.2 = (bf16[264,512]{1,0:T(8,128)(2,1)S(1)}, bf16[264,512]{1,0:T(8,128)(2,1)S(1)}, u32[]{:S(2)}, u32[]{:S(2)}) collective-permute-start(bf16[264,512]{1,0:T(8,128)(2,1)S(1)} %broadcast_dynamic-update-slice_fusion.refs_2_), channel_id=1, source_target_pairs={{112,124},{240,252},{368,380},{496,508},{113,125},{241,253},{369,3... | collective-permute-start | bytes 811016 | tf_op jit(solution)/shard_map/ppermute | solution.py:21
  10.1 13.0 %collective-permute-done.3.refs_2_ = bf16[264,512]{1,0:T(8,128)(2,1)S(1)} collective-permute-done((bf16[264,512]{1,0:T(8,128)(2,1)S(1)}, bf16[264,512]{1,0:T(8,128)(2,1)S(1)}, u32[]{:S(2)}, u32[]{:S(2)}) %collective-permute-start.3) | collective-permute-done | bytes 270368 | tf_op jit(solution)/shard_map/ppermute | solution.py:21
  23.1 5.6 %collective-permute-start.4 = (bf16[264,512]{1,0:T(8,128)(2,1)S(1)}, bf16[264,512]{1,0:T(8,128)(2,1)S(1)}, u32[]{:S(2)}, u32[]{:S(2)}) collective-permute-start(bf16[264,512]{1,0:T(8,128)(2,1)S(1)} %collective-permute-done.3.refs_2_), channel_id=1, source_target_pairs={{0,4},{4,8},{8,12},{12,16},{16,20},{20,24},{24,28},{28,32},{32,36}... | collective-permute-start | bytes 811016 | tf_op jit(solution)/shard_map/ppermute | solution.py:21
  28.7 0.2 collective-permute-done.refs_2_
  28.9 1.9 %collective-permute-start.1 = (bf16[264,512]{1,0:T(8,128)(2,1)S(1)}, bf16[264,512]{1,0:T(8,128)(2,1)S(1)}, u32[]{:S(2)}, u32[]{:S(2)}) collective-permute-start(bf16[264,512]{1,0:T(8,128)(2,1)S(1)} %collective-permute-done.refs_2_), channel_id=1, source_target_pairs={{4,0},{8,4},{12,8},{16,12},{20,16},{24,20},{28,24},{32,28},{36,32}... | collective-permute-start | bytes 811016 | tf_op jit(solution)/shard_map/ppermute | solution.py:21
  30.8 0.1 copy.9.refs_1_
  31.0 0.0 copy-done
  31.0 1.0 %shard_map.46 = (f32[256,1024]{1,0:T(8,128)S(1)}, f32[256,1024]{1,0:T(8,128)S(1)}, f32[256,1024]{1,0:T(8,128)S(1)}) custom-call(bf16[256,1024]{1,0:T(8,128)(2,1)S(1)} %copy-done, f32[256,1]{1,0:T(8,128)S(1)} %copy.9.refs_1_, bf16[264,512]{1,0:T(8,128)(2,1)S(1)} %broadcast_dynamic-update-slice_fusion.refs_2_), custom_call_target="tpu_custom_call" | custom-call | flops 268435456 | bytes 786432 | tf_op jit(solution)/shard_map/pallas_call | solution.py:126
  31.9 1.2 %shard_map.47 = (f32[256,1024]{1,0:T(8,128)S(1)}, f32[256,1024]{1,0:T(8,128)S(1)}, f32[256,1024]{1,0:T(8,128)S(1)}) custom-call(bf16[256,1024]{1,0:T(8,128)(2,1)S(1)} %copy-done, f32[256,1]{1,0:T(8,128)S(1)} %copy.9.refs_1_, bf16[264,512]{1,0:T(8,128)(2,1)S(1)} %collective-permute-done.3.refs_2_, f32[256,1024]{1,0:T(8,128)S(1)} %get-tuple-element.21.refs_3_, ...), custom_call_target="tpu_custom_call" | custom-call | flops 268435456 | bytes 786432 | tf_op jit(solution)/shard_map/pallas_call | solution.py:126
  33.2 0.0 collective-permute-done.5.refs_3_
  33.2 1.4 %shard_map.48 = (f32[256,1024]{1,0:T(8,128)S(1)}, f32[256,1024]{1,0:T(8,128)S(1)}, f32[256,1024]{1,0:T(8,128)S(1)}) custom-call(bf16[256,1024]{1,0:T(8,128)(2,1)S(1)} %copy-done, f32[256,1]{1,0:T(8,128)S(1)} %copy.9.refs_1_, bf16[264,512]{1,0:T(8,128)(2,1)S(1)} %collective-permute-done.refs_2_, bf16[264,512]{1,0:T(8,128)(2,1)S(1)} %collective-permute-done.5.refs_3_, ...), custom_call_target="tpu_custom_call" | custom-call | flops 268435456 | bytes 786432 | tf_op jit(solution)/shard_map/pallas_call | solution.py:126
  34.6 0.0 collective-permute-done.4.refs_2_
  34.6 1.2 %shard_map.49 = (f32[256,1024]{1,0:T(8,128)S(1)}, f32[256,1024]{1,0:T(8,128)S(1)}, f32[256,1024]{1,0:T(8,128)S(1)}) custom-call(bf16[256,1024]{1,0:T(8,128)(2,1)S(1)} %copy-done, f32[256,1]{1,0:T(8,128)S(1)} %copy.9.refs_1_, bf16[264,512]{1,0:T(8,128)(2,1)S(1)} %collective-permute-done.4.refs_2_, f32[256,1024]{1,0:T(8,128)S(1)} %get-tuple-element.27.refs_3_, ...), custom_call_target="tpu_custom_call" | custom-call | flops 268435456 | bytes 786432 | tf_op jit(solution)/shard_map/pallas_call | solution.py:126
  35.8 0.0 collective-permute-done.2.refs_3_
  35.8 3.3 %collective-permute-done.1.refs_2_ = bf16[264,512]{1,0:T(8,128)(2,1)S(1)} collective-permute-done((bf16[264,512]{1,0:T(8,128)(2,1)S(1)}, bf16[264,512]{1,0:T(8,128)(2,1)S(1)}, u32[]{:S(2)}, u32[]{:S(2)}) %collective-permute-start.1) | collective-permute-done | bytes 270368 | tf_op jit(solution)/shard_map/ppermute | solution.py:21
  39.1 2.1 %shard_map.50 = bf16[256,1024]{1,0:T(8,128)(2,1)} custom-call(bf16[256,1024]{1,0:T(8,128)(2,1)S(1)} %copy-done, f32[256,1]{1,0:T(8,128)S(1)} %copy.9.refs_1_, bf16[264,512]{1,0:T(8,128)(2,1)S(1)} %collective-permute-done.1.refs_2_, bf16[264,512]{1,0:T(8,128)(2,1)S(1)} %collective-permute-done.2.refs_3_, f32[256,1024]{1,0:T(8,128)S(1)} %get-tuple-element.30.refs_4_, ...), custom_call_target="tpu_custom_call" | custom-call | flops 268435456 | bytes 786432 | tf_op jit(solution)/shard_map/pallas_call | solution.py:126
  (3 shorter events, 0.0 us)
Async XLA Ops:
  0.0 1.1 %copy-start.1 = (s32[256]{0:T(256)S(1)}, s32[256]{0:T(256)}, u32[]{:S(2)}) copy-start(s32[256]{0:T(256)} %param.7) | copy-start | bytes 3076
  0.0 31.0 %copy-start = (bf16[256,1024]{1,0:T(8,128)(2,1)S(1)}, bf16[256,1024]{1,0:T(8,128)(2,1)}, u32[]{:S(2)}) copy-start(bf16[256,1024]{1,0:T(8,128)(2,1)} %refs_0_.9) | copy-start | bytes 1572868
  1.1 22.0 %collective-permute-start.3 = (bf16[264,512]{1,0:T(8,128)(2,1)S(1)}, bf16[264,512]{1,0:T(8,128)(2,1)S(1)}, u32[]{:S(2)}, u32[]{:S(2)}) collective-permute-start(bf16[264,512]{1,0:T(8,128)(2,1)S(1)} %broadcast_dynamic-update-slice_fusion.refs_2_), channel_id=1, source_target_pairs={{0,4},{4,8},{8,12},{12,16},{16,20},{20,24},{24,28},{28,32},{32,36}... | collective-permute-start | bytes 811016 | tf_op jit(solution)/shard_map/ppermute | solution.py:21
  5.8 23.1 %collective-permute-start = (bf16[264,512]{1,0:T(8,128)(2,1)S(1)}, bf16[264,512]{1,0:T(8,128)(2,1)S(1)}, u32[]{:S(2)}, u32[]{:S(2)}) collective-permute-start(bf16[264,512]{1,0:T(8,128)(2,1)S(1)} %broadcast_dynamic-update-slice_fusion.refs_2_), channel_id=1, source_target_pairs={{0,16},{4,20},{8,24},{12,28},{16,32},{20,36},{24,40},{28,44},{32,4... | collective-permute-start | bytes 811016 | tf_op jit(solution)/shard_map/ppermute | solution.py:21
  8.7 24.4 %collective-permute-start.5 = (bf16[264,512]{1,0:T(8,128)(2,1)S(1)}, bf16[264,512]{1,0:T(8,128)(2,1)S(1)}, u32[]{:S(2)}, u32[]{:S(2)}) collective-permute-start(bf16[264,512]{1,0:T(8,128)(2,1)S(1)} %broadcast_dynamic-update-slice_fusion.refs_2_), channel_id=1, source_target_pairs={{112,128},{240,256},{368,384},{113,129},{241,257},{369,385},{114,1... | collective-permute-start | bytes 811016 | tf_op jit(solution)/shard_map/ppermute | solution.py:21
  9.4 26.4 %collective-permute-start.2 = (bf16[264,512]{1,0:T(8,128)(2,1)S(1)}, bf16[264,512]{1,0:T(8,128)(2,1)S(1)}, u32[]{:S(2)}, u32[]{:S(2)}) collective-permute-start(bf16[264,512]{1,0:T(8,128)(2,1)S(1)} %broadcast_dynamic-update-slice_fusion.refs_2_), channel_id=1, source_target_pairs={{112,124},{240,252},{368,380},{496,508},{113,125},{241,253},{369,3... | collective-permute-start | bytes 811016 | tf_op jit(solution)/shard_map/ppermute | solution.py:21
  23.1 11.5 %collective-permute-start.4 = (bf16[264,512]{1,0:T(8,128)(2,1)S(1)}, bf16[264,512]{1,0:T(8,128)(2,1)S(1)}, u32[]{:S(2)}, u32[]{:S(2)}) collective-permute-start(bf16[264,512]{1,0:T(8,128)(2,1)S(1)} %collective-permute-done.3.refs_2_), channel_id=1, source_target_pairs={{0,4},{4,8},{8,12},{12,16},{16,20},{20,24},{24,28},{28,32},{32,36}... | collective-permute-start | bytes 811016 | tf_op jit(solution)/shard_map/ppermute | solution.py:21
  28.9 10.2 %collective-permute-start.1 = (bf16[264,512]{1,0:T(8,128)(2,1)S(1)}, bf16[264,512]{1,0:T(8,128)(2,1)S(1)}, u32[]{:S(2)}, u32[]{:S(2)}) collective-permute-start(bf16[264,512]{1,0:T(8,128)(2,1)S(1)} %collective-permute-done.refs_2_), channel_id=1, source_target_pairs={{4,0},{8,4},{12,8},{16,12},{20,16},{24,20},{28,24},{32,28},{36,32}... | collective-permute-start | bytes 811016 | tf_op jit(solution)/shard_map/ppermute | solution.py:21

commit v4 on v3

--- a/solution.py
+++ b/solution.py
@@ -57,10 +57,11 @@
             allowed = allowed & (col <= row)
         biases.append(jnp.where(allowed, 0.0, MASKED).astype(jnp.float32))
     copies = []
-    for head in range(q_heads):
-        kv = head // group
-        lanes = slice(head * HEAD_WIDTH, (head + 1) * HEAD_WIDTH)
-        q = q_ref[:, lanes]
+    stacked = group * rows
+    for kv in range(kv_heads):
+        heads = range(kv * group, (kv + 1) * group)
+        span = slice(kv * stacked, (kv + 1) * stacked)
+        q = jnp.concatenate([q_ref[:, h * HEAD_WIDTH : (h + 1) * HEAD_WIDTH] for h in heads], axis=0)
         scores = []
         top = None
         for packet, bias in zip(packets, biases):
@@ -68,17 +69,18 @@
             s = lax.dot_general(
                 q, k, (((1,), (1,)), ((), ())), preferred_element_type=jnp.float32
             )
-            s = s * SCORE_SCALE + bias
+            s = s.reshape(group, rows, rows) * SCORE_SCALE + bias[None]
+            s = s.reshape(stacked, rows)
             scores.append(s)
             m = jnp.max(s, axis=1, keepdims=True)
             top = m if top is None else jnp.maximum(top, m)
-        top = jnp.broadcast_to(top, (rows, HEAD_WIDTH))
+        top = jnp.broadcast_to(top, (stacked, HEAD_WIDTH))
         if prev is not None:
-            old_top = prev[1][:, lanes]
+            old_top = prev[1][span, :]
             top = jnp.maximum(top, old_top)
             fade = jnp.exp2(old_top - top)
-            den = prev[2][:, lanes] * fade
-            num = prev[0][:, lanes] * fade
+            den = prev[2][span, :] * fade
+            num = prev[0][span, :] * fade
         else:
             den = num = None
         wide_top = jnp.concatenate([top] * (rows // HEAD_WIDTH), axis=1)
@@ -93,15 +95,18 @@
             num = add if num is None else num + add
         if final:
             out_ref, held, sems = rest
-            held[:, lanes] = (num * (1.0 / den)).astype(jnp.bfloat16)
-            copies.append(
-                pltpu.make_async_copy(held.at[:, lanes], out_ref.at[:, lanes], sems.at[head])
-            )
-            copies[-1].start()
+            done = (num * (1.0 / den)).astype(jnp.bfloat16)
+            for place, head in enumerate(heads):
+                lanes = slice(head * HEAD_WIDTH, (head + 1) * HEAD_WIDTH)
+                held[:, lanes] = done[place * rows : (place + 1) * rows]
+                copies.append(
+                    pltpu.make_async_copy(held.at[:, lanes], out_ref.at[:, lanes], sems.at[head])
+                )
+                copies[-1].start()
         else:
-            rest[0][:, lanes] = num
-            rest[1][:, lanes] = top
-            rest[2][:, lanes] = den
+            rest[0][span, :] = num
+            rest[1][span, :] = top
+            rest[2][span, :] = den
     for copy in copies:
         copy.wait()
 
@@ -120,7 +125,7 @@
             ],
         )
     else:
-        out_shape = (jax.ShapeDtypeStruct((rows, cols), jnp.float32),) * 3
+        out_shape = (jax.ShapeDtypeStruct((rows * q_heads, HEAD_WIDTH), jnp.float32),) * 3
     args = [queries, q_docs, *[part for packet in packets for part in packet], *(state or ())]
     work = len(packets) * rows * rows * q_heads
     return pl.pallas_call(

time: 41.4 us -> 41.2 us (level)
  Pallas kernels: 6.9 us -> 6.32 us
    pallas_call x5, Pallas kernels: 6.9 us -> 6.32 us  [fold(): pl.pallas_call(functools.partial(attend, [len(packet) for packet in packe...]
  transfers between devices with their start and end apart: 6 -> 6, of which waited for: 3 -> 3; matrix products, arithmetic and copies ran while one was open for 0% -> 0% of each run, Pallas kernels for 12% -> 11%
where the time goes in v4:
time: 41.2 us; the launch traced here: 41 us
  waiting for transfers between devices  16.8 us (41%)
  starting transfers between devices  16.5 us (40%)
  Pallas kernels  6.32 us (15%)
  other arithmetic  1.06 us (3%)
    ppermute x6, waiting for transfers between devices, shifted(): return lax.ppermute(value, 'blk', [pair for pair in pairs if kept(pair[0])])  16.8 us
    ppermute x6, starting transfers between devices, shifted(): return lax.ppermute(value, 'blk', [pair for pair in pairs if kept(pair[0])])  16.5 us
    pallas_call x5, Pallas kernels, fold(): pl.pallas_call(functools.partial(attend, [len(packet) for packet in packe...  6.32 us
    concatenate x1, other arithmetic, pack(): packet = jnp.concatenate([keys, values], axis=1)  1.04 us
  transfers between devices with their start and end apart: 6, of which 3 were waited for; matrix products, arithmetic and copies ran while one was open for 0% of the time, Pallas kernels for 11%

profile of v4, /device:TPU:286, one launch (start us, length us, event | category | flops | bytes accessed | tf_op | source)
XLA Modules:
  0.0 41.0 jit_solution(16359268143028302285)
XLA Ops:
  0.0 0.0 copy-start.1
  0.0 0.0 copy-start
  0.0 1.0 %fusion.2 = bf16[264,512]{1,0:T(8,128)(2,1)S(1)} fusion(bf16[256,256]{1,0:T(8,128)(2,1)} %param.6, bf16[256,256]{1,0:T(8,128)(2,1)} %param.5), kind=kLoop, calls=%fused_computation.3 | loop fusion | flops 946176 | bytes 532480 | tf_op jit(solution)/shard_map/concatenate | solution.py:144
  1.1 0.0 copy-done.1
  1.1 4.7 %collective-permute-start.3 = (bf16[264,512]{1,0:T(8,128)(2,1)S(1)}, bf16[264,512]{1,0:T(8,128)(2,1)S(1)}, u32[]{:S(2)}, u32[]{:S(2)}) collective-permute-start(bf16[264,512]{1,0:T(8,128)(2,1)S(1)} %broadcast_dynamic-update-slice_fusion.refs_2_), channel_id=1, source_target_pairs={{0,4},{4,8},{8,12},{12,16},{16,20},{20,24},{24,28},{28,32},{32,36}... | collective-permute-start | bytes 811016 | tf_op jit(solution)/shard_map/ppermute | solution.py:21
  5.8 2.9 %collective-permute-start = (bf16[264,512]{1,0:T(8,128)(2,1)S(1)}, bf16[264,512]{1,0:T(8,128)(2,1)S(1)}, u32[]{:S(2)}, u32[]{:S(2)}) collective-permute-start(bf16[264,512]{1,0:T(8,128)(2,1)S(1)} %broadcast_dynamic-update-slice_fusion.refs_2_), channel_id=1, source_target_pairs={{0,16},{4,20},{8,24},{12,28},{16,32},{20,36},{24,40},{28,44},{32,4... | collective-permute-start | bytes 811016 | tf_op jit(solution)/shard_map/ppermute | solution.py:21
  8.7 0.7 %collective-permute-start.5 = (bf16[264,512]{1,0:T(8,128)(2,1)S(1)}, bf16[264,512]{1,0:T(8,128)(2,1)S(1)}, u32[]{:S(2)}, u32[]{:S(2)}) collective-permute-start(bf16[264,512]{1,0:T(8,128)(2,1)S(1)} %broadcast_dynamic-update-slice_fusion.refs_2_), channel_id=1, source_target_pairs={{112,128},{240,256},{368,384},{113,129},{241,257},{369,385},{114,1... | collective-permute-start | bytes 811016 | tf_op jit(solution)/shard_map/ppermute | solution.py:21
  9.4 0.7 %collective-permute-start.2 = (bf16[264,512]{1,0:T(8,128)(2,1)S(1)}, bf16[264,512]{1,0:T(8,128)(2,1)S(1)}, u32[]{:S(2)}, u32[]{:S(2)}) collective-permute-start(bf16[264,512]{1,0:T(8,128)(2,1)S(1)} %broadcast_dynamic-update-slice_fusion.refs_2_), channel_id=1, source_target_pairs={{112,124},{240,252},{368,380},{496,508},{113,125},{241,253},{369,3... | collective-permute-start | bytes 811016 | tf_op jit(solution)/shard_map/ppermute | solution.py:21
  10.1 13.0 %collective-permute-done.3.refs_2_ = bf16[264,512]{1,0:T(8,128)(2,1)S(1)} collective-permute-done((bf16[264,512]{1,0:T(8,128)(2,1)S(1)}, bf16[264,512]{1,0:T(8,128)(2,1)S(1)}, u32[]{:S(2)}, u32[]{:S(2)}) %collective-permute-start.3) | collective-permute-done | bytes 270368 | tf_op jit(solution)/shard_map/ppermute | solution.py:21
  23.1 5.6 %collective-permute-start.4 = (bf16[264,512]{1,0:T(8,128)(2,1)S(1)}, bf16[264,512]{1,0:T(8,128)(2,1)S(1)}, u32[]{:S(2)}, u32[]{:S(2)}) collective-permute-start(bf16[264,512]{1,0:T(8,128)(2,1)S(1)} %collective-permute-done.3.refs_2_), channel_id=1, source_target_pairs={{0,4},{4,8},{8,12},{12,16},{16,20},{20,24},{24,28},{28,32},{32,36}... | collective-permute-start | bytes 811016 | tf_op jit(solution)/shard_map/ppermute | solution.py:21
  28.7 0.2 collective-permute-done.refs_2_
  28.9 1.9 %collective-permute-start.1 = (bf16[264,512]{1,0:T(8,128)(2,1)S(1)}, bf16[264,512]{1,0:T(8,128)(2,1)S(1)}, u32[]{:S(2)}, u32[]{:S(2)}) collective-permute-start(bf16[264,512]{1,0:T(8,128)(2,1)S(1)} %collective-permute-done.refs_2_), channel_id=1, source_target_pairs={{4,0},{8,4},{12,8},{16,12},{20,16},{24,20},{28,24},{32,28},{36,32}... | collective-permute-start | bytes 811016 | tf_op jit(solution)/shard_map/ppermute | solution.py:21
  30.8 0.1 copy.9.refs_1_
  31.0 0.0 copy-done
  31.0 1.0 %shard_map.46 = (f32[2048,128]{1,0:T(8,128)S(1)}, f32[2048,128]{1,0:T(8,128)S(1)}, f32[2048,128]{1,0:T(8,128)S(1)}) custom-call(bf16[256,1024]{1,0:T(8,128)(2,1)S(1)} %copy-done, f32[256,1]{1,0:T(8,128)S(1)} %copy.9.refs_1_, bf16[264,512]{1,0:T(8,128)(2,1)S(1)} %broadcast_dynamic-update-slice_fusion.refs_2_), custom_call_target="tpu_custom_call" | custom-call | flops 268435456 | bytes 786432 | tf_op jit(solution)/shard_map/pallas_call | solution.py:131
  31.9 1.2 %shard_map.47 = (f32[2048,128]{1,0:T(8,128)S(1)}, f32[2048,128]{1,0:T(8,128)S(1)}, f32[2048,128]{1,0:T(8,128)S(1)}) custom-call(bf16[256,1024]{1,0:T(8,128)(2,1)S(1)} %copy-done, f32[256,1]{1,0:T(8,128)S(1)} %copy.9.refs_1_, bf16[264,512]{1,0:T(8,128)(2,1)S(1)} %collective-permute-done.3.refs_2_, f32[2048,128]{1,0:T(8,128)S(1)} %get-tuple-element.21.refs_3_, ...), custom_call_target="tpu_custom_call" | custom-call | flops 268435456 | bytes 786432 | tf_op jit(solution)/shard_map/pallas_call | solution.py:131
  33.1 0.0 collective-permute-done.5.refs_3_
  33.1 1.1 %shard_map.48 = (f32[2048,128]{1,0:T(8,128)S(1)}, f32[2048,128]{1,0:T(8,128)S(1)}, f32[2048,128]{1,0:T(8,128)S(1)}) custom-call(bf16[256,1024]{1,0:T(8,128)(2,1)S(1)} %copy-done, f32[256,1]{1,0:T(8,128)S(1)} %copy.9.refs_1_, bf16[264,512]{1,0:T(8,128)(2,1)S(1)} %collective-permute-done.refs_2_, bf16[264,512]{1,0:T(8,128)(2,1)S(1)} %collective-permute-done.5.refs_3_, ...), custom_call_target="tpu_custom_call" | custom-call | flops 268435456 | bytes 786432 | tf_op jit(solution)/shard_map/pallas_call | solution.py:131
  34.3 0.0 collective-permute-done.4.refs_2_
  34.3 1.2 %shard_map.49 = (f32[2048,128]{1,0:T(8,128)S(1)}, f32[2048,128]{1,0:T(8,128)S(1)}, f32[2048,128]{1,0:T(8,128)S(1)}) custom-call(bf16[256,1024]{1,0:T(8,128)(2,1)S(1)} %copy-done, f32[256,1]{1,0:T(8,128)S(1)} %copy.9.refs_1_, bf16[264,512]{1,0:T(8,128)(2,1)S(1)} %collective-permute-done.4.refs_2_, f32[2048,128]{1,0:T(8,128)S(1)} %get-tuple-element.27.refs_3_, ...), custom_call_target="tpu_custom_call" | custom-call | flops 268435456 | bytes 786432 | tf_op jit(solution)/shard_map/pallas_call | solution.py:131
  35.5 0.0 collective-permute-done.2.refs_3_
  35.5 3.6 %collective-permute-done.1.refs_2_ = bf16[264,512]{1,0:T(8,128)(2,1)S(1)} collective-permute-done((bf16[264,512]{1,0:T(8,128)(2,1)S(1)}, bf16[264,512]{1,0:T(8,128)(2,1)S(1)}, u32[]{:S(2)}, u32[]{:S(2)}) %collective-permute-start.1) | collective-permute-done | bytes 270368 | tf_op jit(solution)/shard_map/ppermute | solution.py:21
  39.1 1.9 %shard_map.50 = bf16[256,1024]{1,0:T(8,128)(2,1)} custom-call(bf16[256,1024]{1,0:T(8,128)(2,1)S(1)} %copy-done, f32[256,1]{1,0:T(8,128)S(1)} %copy.9.refs_1_, bf16[264,512]{1,0:T(8,128)(2,1)S(1)} %collective-permute-done.1.refs_2_, bf16[264,512]{1,0:T(8,128)(2,1)S(1)} %collective-permute-done.2.refs_3_, f32[2048,128]{1,0:T(8,128)S(1)} %get-tuple-element.30.refs_4_, ...), custom_call_target="tpu_custom_call" | custom-call | flops 268435456 | bytes 786432 | tf_op jit(solution)/shard_map/pallas_call | solution.py:131
  (3 shorter events, 0.0 us)
Async XLA Ops:
  0.0 1.1 %copy-start.1 = (s32[256]{0:T(256)S(1)}, s32[256]{0:T(256)}, u32[]{:S(2)}) copy-start(s32[256]{0:T(256)} %param.7) | copy-start | bytes 3076
  0.0 31.0 %copy-start = (bf16[256,1024]{1,0:T(8,128)(2,1)S(1)}, bf16[256,1024]{1,0:T(8,128)(2,1)}, u32[]{:S(2)}) copy-start(bf16[256,1024]{1,0:T(8,128)(2,1)} %refs_0_.9) | copy-start | bytes 1572868
  1.1 22.0 %collective-permute-start.3 = (bf16[264,512]{1,0:T(8,128)(2,1)S(1)}, bf16[264,512]{1,0:T(8,128)(2,1)S(1)}, u32[]{:S(2)}, u32[]{:S(2)}) collective-permute-start(bf16[264,512]{1,0:T(8,128)(2,1)S(1)} %broadcast_dynamic-update-slice_fusion.refs_2_), channel_id=1, source_target_pairs={{0,4},{4,8},{8,12},{12,16},{16,20},{20,24},{24,28},{28,32},{32,36}... | collective-permute-start | bytes 811016 | tf_op jit(solution)/shard_map/ppermute | solution.py:21
  5.8 23.1 %collective-permute-start = (bf16[264,512]{1,0:T(8,128)(2,1)S(1)}, bf16[264,512]{1,0:T(8,128)(2,1)S(1)}, u32[]{:S(2)}, u32[]{:S(2)}) collective-permute-start(bf16[264,512]{1,0:T(8,128)(2,1)S(1)} %broadcast_dynamic-update-slice_fusion.refs_2_), channel_id=1, source_target_pairs={{0,16},{4,20},{8,24},{12,28},{16,32},{20,36},{24,40},{28,44},{32,4... | collective-permute-start | bytes 811016 | tf_op jit(solution)/shard_map/ppermute | solution.py:21
  8.7 24.4 %collective-permute-start.5 = (bf16[264,512]{1,0:T(8,128)(2,1)S(1)}, bf16[264,512]{1,0:T(8,128)(2,1)S(1)}, u32[]{:S(2)}, u32[]{:S(2)}) collective-permute-start(bf16[264,512]{1,0:T(8,128)(2,1)S(1)} %broadcast_dynamic-update-slice_fusion.refs_2_), channel_id=1, source_target_pairs={{112,128},{240,256},{368,384},{113,129},{241,257},{369,385},{114,1... | collective-permute-start | bytes 811016 | tf_op jit(solution)/shard_map/ppermute | solution.py:21
  9.4 26.1 %collective-permute-start.2 = (bf16[264,512]{1,0:T(8,128)(2,1)S(1)}, bf16[264,512]{1,0:T(8,128)(2,1)S(1)}, u32[]{:S(2)}, u32[]{:S(2)}) collective-permute-start(bf16[264,512]{1,0:T(8,128)(2,1)S(1)} %broadcast_dynamic-update-slice_fusion.refs_2_), channel_id=1, source_target_pairs={{112,124},{240,252},{368,380},{496,508},{113,125},{241,253},{369,3... | collective-permute-start | bytes 811016 | tf_op jit(solution)/shard_map/ppermute | solution.py:21
  23.1 11.2 %collective-permute-start.4 = (bf16[264,512]{1,0:T(8,128)(2,1)S(1)}, bf16[264,512]{1,0:T(8,128)(2,1)S(1)}, u32[]{:S(2)}, u32[]{:S(2)}) collective-permute-start(bf16[264,512]{1,0:T(8,128)(2,1)S(1)} %collective-permute-done.3.refs_2_), channel_id=1, source_target_pairs={{0,4},{4,8},{8,12},{12,16},{16,20},{20,24},{24,28},{28,32},{32,36}... | collective-permute-start | bytes 811016 | tf_op jit(solution)/shard_map/ppermute | solution.py:21
  28.9 10.2 %collective-permute-start.1 = (bf16[264,512]{1,0:T(8,128)(2,1)S(1)}, bf16[264,512]{1,0:T(8,128)(2,1)S(1)}, u32[]{:S(2)}, u32[]{:S(2)}) collective-permute-start(bf16[264,512]{1,0:T(8,128)(2,1)S(1)} %collective-permute-done.refs_2_), channel_id=1, source_target_pairs={{4,0},{8,4},{12,8},{16,12},{20,16},{24,20},{28,24},{32,28},{36,32}... | collective-permute-start | bytes 811016 | tf_op jit(solution)/shard_map/ppermute | solution.py:21

commit v5 on v4

--- a/solution.py
+++ b/solution.py
@@ -57,10 +57,12 @@
             allowed = allowed & (col <= row)
         biases.append(jnp.where(allowed, 0.0, MASKED).astype(jnp.float32))
     copies = []
-    stacked = group * rows
-    for kv in range(kv_heads):
-        heads = range(kv * group, (kv + 1) * group)
-        span = slice(kv * stacked, (kv + 1) * stacked)
+    step = group // 2 if final and group % 2 == 0 else group
+    stacked = step * rows
+    for start in range(0, q_heads, step):
+        kv = start // group
+        heads = range(start, start + step)
+        span = slice(start * rows, (start + step) * rows)
         q = jnp.concatenate([q_ref[:, h * HEAD_WIDTH : (h + 1) * HEAD_WIDTH] for h in heads], axis=0)
         scores = []
         top = None
@@ -69,7 +71,7 @@
             s = lax.dot_general(
                 q, k, (((1,), (1,)), ((), ())), preferred_element_type=jnp.float32
             )
-            s = s.reshape(group, rows, rows) * SCORE_SCALE + bias[None]
+            s = s.reshape(step, rows, rows) * SCORE_SCALE + bias[None]
             s = s.reshape(stacked, rows)
             scores.append(s)
             m = jnp.max(s, axis=1, keepdims=True)
@@ -161,9 +163,9 @@
     three = shifted(four, -1, lambda source: source % PLANE != 0)
     state = fold(queries, q_docs, [[packet]], None, False)
     state = fold(queries, q_docs, [[one]], state, False)
-    state = fold(queries, q_docs, [[four, far_four]], state, False)
+    state = fold(queries, q_docs, [[four], [far_four, far_three]], state, False)
     state = fold(queries, q_docs, [[two]], state, False)
-    return fold(queries, q_docs, [[three, far_three]], state, True)
+    return fold(queries, q_docs, [[three]], state, True)
 
 
 def solution(mesh):

time: 41.2 us -> 41.2 us (level)
  Pallas kernels: 6.32 us -> 7.33 us
  waiting for transfers between devices: 16.8 us -> 15.9 us
    pallas_call x5, Pallas kernels: 6.32 us -> 7.33 us  [fold(): pl.pallas_call(functools.partial(attend, [len(packet) for packet in packe...]
    ppermute x6, waiting for transfers between devices: 16.8 us -> 15.9 us  [shifted(): return lax.ppermute(value, 'blk', [pair for pair in pairs if kept(pair[0])])]
  transfers between devices with their start and end apart: 6 -> 6, of which waited for: 3 -> 3; matrix products, arithmetic and copies ran while one was open for 0% -> 0% of each run, Pallas kernels for 11% -> 13%
where the time goes in v5:
time: 41.2 us; the launch traced here: 41 us
  starting transfers between devices  16.5 us (40%)
  waiting for transfers between devices  15.9 us (39%)
  Pallas kernels  7.33 us (18%)
  other arithmetic  1.06 us (3%)
    ppermute x6, starting transfers between devices, shifted(): return lax.ppermute(value, 'blk', [pair for pair in pairs if kept(pair[0])])  16.5 us
    ppermute x6, waiting for transfers between devices, shifted(): return lax.ppermute(value, 'blk', [pair for pair in pairs if kept(pair[0])])  15.9 us
    pallas_call x5, Pallas kernels, fold(): pl.pallas_call(functools.partial(attend, [len(packet) for packet in packe...  7.33 us
    concatenate x1, other arithmetic, pack(): packet = jnp.concatenate([keys, values], axis=1)  1.04 us
  transfers between devices with their start and end apart: 6, of which 3 were waited for; matrix products, arithmetic and copies ran while one was open for 0% of the time, Pallas kernels for 13%

profile of v5, /device:TPU:286, one launch (start us, length us, event | category | flops | bytes accessed | tf_op | source)
XLA Modules:
  0.0 41.0 jit_solution(16997550785206403715)
XLA Ops:
  0.0 0.0 copy-start.1
  0.0 0.0 copy-start
  0.0 1.0 %fusion.2 = bf16[264,512]{1,0:T(8,128)(2,1)S(1)} fusion(bf16[256,256]{1,0:T(8,128)(2,1)} %param.6, bf16[256,256]{1,0:T(8,128)(2,1)} %param.5), kind=kLoop, calls=%fused_computation.3 | loop fusion | flops 946176 | bytes 532480 | tf_op jit(solution)/shard_map/concatenate | solution.py:146
  1.1 0.0 copy-done.1
  1.1 4.7 %collective-permute-start.2 = (bf16[264,512]{1,0:T(8,128)(2,1)S(1)}, bf16[264,512]{1,0:T(8,128)(2,1)S(1)}, u32[]{:S(2)}, u32[]{:S(2)}) collective-permute-start(bf16[264,512]{1,0:T(8,128)(2,1)S(1)} %broadcast_dynamic-update-slice_fusion.refs_2_), channel_id=1, source_target_pairs={{0,4},{4,8},{8,12},{12,16},{16,20},{20,24},{24,28},{28,32},{32,36}... | collective-permute-start | bytes 811016 | tf_op jit(solution)/shard_map/ppermute | solution.py:21
  5.8 2.9 %collective-permute-start = (bf16[264,512]{1,0:T(8,128)(2,1)S(1)}, bf16[264,512]{1,0:T(8,128)(2,1)S(1)}, u32[]{:S(2)}, u32[]{:S(2)}) collective-permute-start(bf16[264,512]{1,0:T(8,128)(2,1)S(1)} %broadcast_dynamic-update-slice_fusion.refs_2_), channel_id=1, source_target_pairs={{0,16},{4,20},{8,24},{12,28},{16,32},{20,36},{24,40},{28,44},{32,4... | collective-permute-start | bytes 811016 | tf_op jit(solution)/shard_map/ppermute | solution.py:21
  8.7 0.7 %collective-permute-start.4 = (bf16[264,512]{1,0:T(8,128)(2,1)S(1)}, bf16[264,512]{1,0:T(8,128)(2,1)S(1)}, u32[]{:S(2)}, u32[]{:S(2)}) collective-permute-start(bf16[264,512]{1,0:T(8,128)(2,1)S(1)} %broadcast_dynamic-update-slice_fusion.refs_2_), channel_id=1, source_target_pairs={{112,128},{240,256},{368,384},{113,129},{241,257},{369,385},{114,1... | collective-permute-start | bytes 811016 | tf_op jit(solution)/shard_map/ppermute | solution.py:21
  9.4 0.7 %collective-permute-start.5 = (bf16[264,512]{1,0:T(8,128)(2,1)S(1)}, bf16[264,512]{1,0:T(8,128)(2,1)S(1)}, u32[]{:S(2)}, u32[]{:S(2)}) collective-permute-start(bf16[264,512]{1,0:T(8,128)(2,1)S(1)} %broadcast_dynamic-update-slice_fusion.refs_2_), channel_id=1, source_target_pairs={{112,124},{240,252},{368,380},{496,508},{113,125},{241,253},{369,3... | collective-permute-start | bytes 811016 | tf_op jit(solution)/shard_map/ppermute | solution.py:21
  10.1 13.0 %collective-permute-done.2.refs_2_ = bf16[264,512]{1,0:T(8,128)(2,1)S(1)} collective-permute-done((bf16[264,512]{1,0:T(8,128)(2,1)S(1)}, bf16[264,512]{1,0:T(8,128)(2,1)S(1)}, u32[]{:S(2)}, u32[]{:S(2)}) %collective-permute-start.2) | collective-permute-done | bytes 270368 | tf_op jit(solution)/shard_map/ppermute | solution.py:21
  23.1 5.6 %collective-permute-start.3 = (bf16[264,512]{1,0:T(8,128)(2,1)S(1)}, bf16[264,512]{1,0:T(8,128)(2,1)S(1)}, u32[]{:S(2)}, u32[]{:S(2)}) collective-permute-start(bf16[264,512]{1,0:T(8,128)(2,1)S(1)} %collective-permute-done.2.refs_2_), channel_id=1, source_target_pairs={{0,4},{4,8},{8,12},{12,16},{16,20},{20,24},{24,28},{28,32},{32,36}... | collective-permute-start | bytes 811016 | tf_op jit(solution)/shard_map/ppermute | solution.py:21
  28.7 0.2 collective-permute-done.refs_2_
  28.9 1.9 %collective-permute-start.1 = (bf16[264,512]{1,0:T(8,128)(2,1)S(1)}, bf16[264,512]{1,0:T(8,128)(2,1)S(1)}, u32[]{:S(2)}, u32[]{:S(2)}) collective-permute-start(bf16[264,512]{1,0:T(8,128)(2,1)S(1)} %collective-permute-done.refs_2_), channel_id=1, source_target_pairs={{4,0},{8,4},{12,8},{16,12},{20,16},{24,20},{28,24},{32,28},{36,32}... | collective-permute-start | bytes 811016 | tf_op jit(solution)/shard_map/ppermute | solution.py:21
  30.8 0.1 copy.9.refs_1_
  31.0 0.0 copy-done
  31.0 1.0 %shard_map.46 = (f32[2048,128]{1,0:T(8,128)S(1)}, f32[2048,128]{1,0:T(8,128)S(1)}, f32[2048,128]{1,0:T(8,128)S(1)}) custom-call(bf16[256,1024]{1,0:T(8,128)(2,1)S(1)} %copy-done, f32[256,1]{1,0:T(8,128)S(1)} %copy.9.refs_1_, bf16[264,512]{1,0:T(8,128)(2,1)S(1)} %broadcast_dynamic-update-slice_fusion.refs_2_), custom_call_target="tpu_custom_call" | custom-call | flops 268435456 | bytes 786432 | tf_op jit(solution)/shard_map/pallas_call | solution.py:133
  31.9 1.2 %shard_map.47 = (f32[2048,128]{1,0:T(8,128)S(1)}, f32[2048,128]{1,0:T(8,128)S(1)}, f32[2048,128]{1,0:T(8,128)S(1)}) custom-call(bf16[256,1024]{1,0:T(8,128)(2,1)S(1)} %copy-done, f32[256,1]{1,0:T(8,128)S(1)} %copy.9.refs_1_, bf16[264,512]{1,0:T(8,128)(2,1)S(1)} %collective-permute-done.2.refs_2_, f32[2048,128]{1,0:T(8,128)S(1)} %get-tuple-element.21.refs_3_, ...), custom_call_target="tpu_custom_call" | custom-call | flops 268435456 | bytes 786432 | tf_op jit(solution)/shard_map/pallas_call | solution.py:133
  33.1 0.0 collective-permute-done.4.refs_3_
  33.1 0.0 collective-permute-done.5.refs_4_
  33.1 2.2 %shard_map.48 = (f32[2048,128]{1,0:T(8,128)S(1)}, f32[2048,128]{1,0:T(8,128)S(1)}, f32[2048,128]{1,0:T(8,128)S(1)}) custom-call(bf16[256,1024]{1,0:T(8,128)(2,1)S(1)} %copy-done, f32[256,1]{1,0:T(8,128)S(1)} %copy.9.refs_1_, bf16[264,512]{1,0:T(8,128)(2,1)S(1)} %collective-permute-done.refs_2_, bf16[264,512]{1,0:T(8,128)(2,1)S(1)} %collective-permute-done.4.refs_3_, ...), custom_call_target="tpu_custom_call" | custom-call | flops 536870912 | bytes 786432 | tf_op jit(solution)/shard_map/pallas_call | solution.py:133
  35.3 0.0 collective-permute-done.3.refs_2_
  35.3 1.1 %shard_map.49 = (f32[2048,128]{1,0:T(8,128)S(1)}, f32[2048,128]{1,0:T(8,128)S(1)}, f32[2048,128]{1,0:T(8,128)S(1)}) custom-call(bf16[256,1024]{1,0:T(8,128)(2,1)S(1)} %copy-done, f32[256,1]{1,0:T(8,128)S(1)} %copy.9.refs_1_, bf16[264,512]{1,0:T(8,128)(2,1)S(1)} %collective-permute-done.3.refs_2_, f32[2048,128]{1,0:T(8,128)S(1)} %get-tuple-element.27.refs_3_, ...), custom_call_target="tpu_custom_call" | custom-call | flops 268435456 | bytes 786432 | tf_op jit(solution)/shard_map/pallas_call | solution.py:133
  36.4 2.7 %collective-permute-done.1.refs_2_ = bf16[264,512]{1,0:T(8,128)(2,1)S(1)} collective-permute-done((bf16[264,512]{1,0:T(8,128)(2,1)S(1)}, bf16[264,512]{1,0:T(8,128)(2,1)S(1)}, u32[]{:S(2)}, u32[]{:S(2)}) %collective-permute-start.1) | collective-permute-done | bytes 270368 | tf_op jit(solution)/shard_map/ppermute | solution.py:21
  39.1 1.9 %shard_map.50 = bf16[256,1024]{1,0:T(8,128)(2,1)} custom-call(bf16[256,1024]{1,0:T(8,128)(2,1)S(1)} %copy-done, f32[256,1]{1,0:T(8,128)S(1)} %copy.9.refs_1_, bf16[264,512]{1,0:T(8,128)(2,1)S(1)} %collective-permute-done.1.refs_2_, f32[2048,128]{1,0:T(8,128)S(1)} %get-tuple-element.30.refs_3_, f32[2048,128]{1,0:T(8,128)S(1)} %get-tuple-element.31.refs_4_, ...), custom_call_target="tpu_custom_call" | custom-call | flops 268435456 | bytes 786432 | tf_op jit(solution)/shard_map/pallas_call | solution.py:133
  (3 shorter events, 0.0 us)
Async XLA Ops:
  0.0 1.1 %copy-start.1 = (s32[256]{0:T(256)S(1)}, s32[256]{0:T(256)}, u32[]{:S(2)}) copy-start(s32[256]{0:T(256)} %param.7) | copy-start | bytes 3076
  0.0 31.0 %copy-start = (bf16[256,1024]{1,0:T(8,128)(2,1)S(1)}, bf16[256,1024]{1,0:T(8,128)(2,1)}, u32[]{:S(2)}) copy-start(bf16[256,1024]{1,0:T(8,128)(2,1)} %refs_0_.9) | copy-start | bytes 1572868
  1.1 22.0 %collective-permute-start.2 = (bf16[264,512]{1,0:T(8,128)(2,1)S(1)}, bf16[264,512]{1,0:T(8,128)(2,1)S(1)}, u32[]{:S(2)}, u32[]{:S(2)}) collective-permute-start(bf16[264,512]{1,0:T(8,128)(2,1)S(1)} %broadcast_dynamic-update-slice_fusion.refs_2_), channel_id=1, source_target_pairs={{0,4},{4,8},{8,12},{12,16},{16,20},{20,24},{24,28},{28,32},{32,36}... | collective-permute-start | bytes 811016 | tf_op jit(solution)/shard_map/ppermute | solution.py:21
  5.8 23.1 %collective-permute-start = (bf16[264,512]{1,0:T(8,128)(2,1)S(1)}, bf16[264,512]{1,0:T(8,128)(2,1)S(1)}, u32[]{:S(2)}, u32[]{:S(2)}) collective-permute-start(bf16[264,512]{1,0:T(8,128)(2,1)S(1)} %broadcast_dynamic-update-slice_fusion.refs_2_), channel_id=1, source_target_pairs={{0,16},{4,20},{8,24},{12,28},{16,32},{20,36},{24,40},{28,44},{32,4... | collective-permute-start | bytes 811016 | tf_op jit(solution)/shard_map/ppermute | solution.py:21
  8.7 24.4 %collective-permute-start.4 = (bf16[264,512]{1,0:T(8,128)(2,1)S(1)}, bf16[264,512]{1,0:T(8,128)(2,1)S(1)}, u32[]{:S(2)}, u32[]{:S(2)}) collective-permute-start(bf16[264,512]{1,0:T(8,128)(2,1)S(1)} %broadcast_dynamic-update-slice_fusion.refs_2_), channel_id=1, source_target_pairs={{112,128},{240,256},{368,384},{113,129},{241,257},{369,385},{114,1... | collective-permute-start | bytes 811016 | tf_op jit(solution)/shard_map/ppermute | solution.py:21
  9.4 23.7 %collective-permute-start.5 = (bf16[264,512]{1,0:T(8,128)(2,1)S(1)}, bf16[264,512]{1,0:T(8,128)(2,1)S(1)}, u32[]{:S(2)}, u32[]{:S(2)}) collective-permute-start(bf16[264,512]{1,0:T(8,128)(2,1)S(1)} %broadcast_dynamic-update-slice_fusion.refs_2_), channel_id=1, source_target_pairs={{112,124},{240,252},{368,380},{496,508},{113,125},{241,253},{369,3... | collective-permute-start | bytes 811016 | tf_op jit(solution)/shard_map/ppermute | solution.py:21
  23.1 12.2 %collective-permute-start.3 = (bf16[264,512]{1,0:T(8,128)(2,1)S(1)}, bf16[264,512]{1,0:T(8,128)(2,1)S(1)}, u32[]{:S(2)}, u32[]{:S(2)}) collective-permute-start(bf16[264,512]{1,0:T(8,128)(2,1)S(1)} %collective-permute-done.2.refs_2_), channel_id=1, source_target_pairs={{0,4},{4,8},{8,12},{12,16},{16,20},{20,24},{24,28},{28,32},{32,36}... | collective-permute-start | bytes 811016 | tf_op jit(solution)/shard_map/ppermute | solution.py:21
  28.9 10.2 %collective-permute-start.1 = (bf16[264,512]{1,0:T(8,128)(2,1)S(1)}, bf16[264,512]{1,0:T(8,128)(2,1)S(1)}, u32[]{:S(2)}, u32[]{:S(2)}) collective-permute-start(bf16[264,512]{1,0:T(8,128)(2,1)S(1)} %collective-permute-done.refs_2_), channel_id=1, source_target_pairs={{4,0},{8,4},{12,8},{16,12},{20,16},{24,20},{28,24},{32,28},{36,32}... | collective-permute-start | bytes 811016 | tf_op jit(solution)/shard_map/ppermute | solution.py:21
